TPU v7x, 256 devices: a whole 4x4x8 slice. The times are simulated.
256 devices in a mesh: ctx: 32 (over y_lo, z, core), rep: 8 (over x, y_hi).
Axes of the slice: x: 4, y: 4 (y_hi: 2, y_lo: 2; y = y_hi * 2 + y_lo), z: 8, core: 2. Of those that a mesh axis runs over, the one named last changes fastest.
Arguments:
- q_policy: bfloat16 [32768, 2560], P(('rep', 'ctx')), parts along dimension 0, may hold values from -8 to 8
- kv_policy: bfloat16 [32768, 1024], P(('rep', 'ctx')), parts along dimension 0, may hold values from -8 to 8
- q_ref: bfloat16 [32768, 2560], P(('rep', 'ctx')), parts along dimension 0, may hold values from -8 to 8
- kv_ref: bfloat16 [32768, 1024], P(('rep', 'ctx')), parts along dimension 0, may hold values from -8 to 8
- doc_lengths: int32 [64], P('rep'), parts along dimension 0, may hold values from 1 to 2048, 4096 in all
- span_order: int32 [256], P('rep'), parts along dimension 0, may hold values from 0 to 31, each once
Outputs:
- attn_policy: bfloat16 [32768, 2560], P(('rep', 'ctx')), parts along dimension 0
- attn_ref: bfloat16 [32768, 2560], P(('rep', 'ctx')), parts along dimension 0
There are 8 independent parts, one for each index of `rep`. A program takes and returns all parts, laid end to end along the dimension named above; each array names one. Nothing has to cross between parts.
Inputs may be any that keep to these rules, and one draw needn't show every extreme that they name: `doc_lengths`: the lengths of the rollout's documents in order; they sum to 4096 and the longest has 2048 tokens. Stored block i of 128 rows holds positions span_order[i] * 128 onward in order; every block of positions once.
All inputs are finite; a program needn't handle non-finite values.
Results may differ from a plain program's by a relative error of at most 0.0065.
Values may be sent and summed in bfloat16 or wider, within the bound.
A program may use at most 192 MiB of HBM per device.

v0:
```python
import jax
import jax.numpy as jnp
from jax import lax
from jax.sharding import PartitionSpec as P

HQ = 20
HK = 4
HD = 128


def passed_along(block, axis, distance):
    devices = range(lax.axis_size(axis))
    route = [((i - distance) % len(devices), i) for i in devices]
    return lax.ppermute(block, axis, route)


def on_device(q_policy, kv_policy, q_ref, kv_ref, doc_lengths, span_order):
    tok_rows = q_policy.shape[0]
    count_ctx = lax.axis_size("ctx")
    own_index = lax.axis_index("ctx")
    group_size = HQ // HK
    score_scale = 1.0 / jnp.sqrt(jnp.float32(HD))
    local_rows = jnp.arange(tok_rows, dtype=jnp.int32)
    doc_ends = jnp.cumsum(doc_lengths)
    block_ids = jnp.arange(count_ctx, dtype=jnp.int32)

    def documents(pos_rows):
        return jnp.sum((doc_ends[None, :] <= pos_rows[:, None]).astype(jnp.int32), axis=1)

    def lookup(index_rows):
        return jnp.sum(
            jnp.where(index_rows[:, None] == block_ids[None, :], span_order[None, :], 0), axis=1
        )

    def row_positions(source_rows, inner_rows):
        return lookup(source_rows) * tok_rows + inner_rows

    def positions(source):
        return row_positions(jnp.full((tok_rows,), source, jnp.int32), local_rows)

    q_pos = positions(own_index)
    q_doc = documents(q_pos)
    queries = (
        q_policy.reshape(tok_rows, HK, group_size, HD),
        q_ref.reshape(tok_rows, HK, group_size, HD),
    )

    def update(carry_state, blocks, allowed):
        key_count = blocks.shape[1]
        results = []
        for model in range(2):
            peaks, totals, summed = carry_state[model]
            key_rows = blocks[model, :, : HK * HD].reshape(key_count, HK, HD)
            value_rows = blocks[model, :, HK * HD :].reshape(key_count, HK, HD)
            scores = (
                jnp.einsum(
                    "tkgd,skd->kgts", queries[model], key_rows, preferred_element_type=jnp.float32
                )
                * score_scale
            )
            new_peaks = jnp.maximum(peaks, jnp.max(jnp.where(allowed, scores, -1e30), axis=-1))
            weights = jnp.where(allowed, jnp.exp(scores - new_peaks[..., None]), 0.0)
            shrink = jnp.exp(peaks - new_peaks)
            totals = totals * shrink + jnp.sum(weights, axis=-1)
            mixed_out = jnp.einsum(
                "kgts,skd->tkgd",
                weights.astype(jnp.bfloat16),
                value_rows,
                preferred_element_type=jnp.float32,
            )
            summed = summed * jnp.transpose(shrink, (2, 0, 1))[..., None] + mixed_out
            results.append((new_peaks, totals, summed))
        return (results[0], results[1])

    def attend_at(carry_state, blocks, k_pos):
        k_doc = documents(k_pos)
        allowed = (k_pos[None, :] <= q_pos[:, None]) & (k_doc[None, :] == q_doc[:, None])
        return update(carry_state, blocks, allowed)

    def attend(carry_state, blocks, source):
        return attend_at(carry_state, blocks, positions(source))

    empty_peaks = jnp.full((HK, group_size, tok_rows), -1e30, jnp.float32)
    empty_totals = jnp.zeros((HK, group_size, tok_rows), jnp.float32)
    empty_summed = jnp.zeros((tok_rows, HK, group_size, HD), jnp.float32)
    carry_state = (
        (empty_peaks, empty_totals, empty_summed),
        (empty_peaks, empty_totals, empty_summed),
    )
    blocks = jnp.stack((kv_policy, kv_ref))
    carry_state = attend(carry_state, blocks, own_index)

    def one_turn(turn_index, carry):
        given, moving = carry
        moving = passed_along(moving, "ctx", 1)
        given = attend(given, moving, (own_index - turn_index) % count_ctx)
        return (given, moving)

    carry_state, blocks = lax.fori_loop(1, count_ctx, one_turn, (carry_state, blocks))
    finished = []
    for model in range(2):
        peaks, totals, summed = carry_state[model]
        result = summed / jnp.transpose(totals, (2, 0, 1))[..., None]
        finished.append(result.astype(jnp.bfloat16).reshape(tok_rows, HQ * HD))
    attn_policy, attn_ref = (finished[0], finished[1])
    return (attn_policy, attn_ref)


def solution(mesh):
    in_specs = (
        P(("rep", "ctx"), None),
        P(("rep", "ctx"), None),
        P(("rep", "ctx"), None),
        P(("rep", "ctx"), None),
        P("rep"),
        P("rep"),
    )
    out_specs = (P(("rep", "ctx"), None), P(("rep", "ctx"), None))
    return jax.shard_map(
        on_device, mesh=mesh, in_specs=in_specs, out_specs=out_specs, check_vma=False
    )
```

profile of v0, /device:TPU:1, one launch (start us, length us, event | category | flops | bytes accessed | tf_op | source)
XLA Modules:
  0.0 505.0 jit_solution(3812316780190048541)
XLA Ops:
  2.5 1.1 copy.44
  5.5 0.9 fusion.47
  6.7 1.5 select_reduce_fusion.3
  12.4 1.1 copy.56
  13.5 2.2 copy.57
  15.7 483.6 %while.28 = (s32[]{:T(128)}, f32[4,5,128]{2,1,0:T(8,128)S(1)}, f32[4,5,128]{2,1,0:T(8,128)S(1)}, f32[128,4,5,128]{3,0,2,1:T(8,128)S(1)}, f32[4,5,128]{2,1,0:T(8,...) while((s32[]{:T(128)}, f32[4,5,128]{2,1,0:T(8,128)S(1)}, ...), condition=%wide.region_14.15_spmd.clone, body=%wide.region_7.14_spmd.clone.sunk | while | flops 342829120 | bytes 26104936 | solution.py:99
  15.7 3.0 collective-permute-start
  19.0 6.1 %collective-permute-done = bf16[2,128,1024]{1,2,0:T(8,128)(2,1)S(1)} collective-permute-done((bf16[2,128,1024]{1,2,0:T(8,128)(2,1)}, bf16[2,128,1024]{1,2,0:T(8,128)(2,1)S(1)}, u32[]{:S(2)}, u32[]{:S(2)}) %collective-permute-start) | collective-permute-done | bytes 524320 | tf_op jit(solution)/shard_map/while/body/eval_jaxpr/ppermute | solution.py:14
  27.4 0.9 fusion.90
  28.3 0.9 fusion.89
  30.0 2.4 collective-permute-start
  32.7 6.1 %collective-permute-done = bf16[2,128,1024]{1,2,0:T(8,128)(2,1)S(1)} collective-permute-done((bf16[2,128,1024]{1,2,0:T(8,128)(2,1)}, bf16[2,128,1024]{1,2,0:T(8,128)(2,1)S(1)}, u32[]{:S(2)}, u32[]{:S(2)}) %collective-permute-start) | collective-permute-done | bytes 524320 | tf_op jit(solution)/shard_map/while/body/eval_jaxpr/ppermute | solution.py:14
  41.1 0.9 fusion.90
  42.0 0.9 fusion.89
  43.7 2.4 collective-permute-start
  46.3 6.5 %collective-permute-done = bf16[2,128,1024]{1,2,0:T(8,128)(2,1)S(1)} collective-permute-done((bf16[2,128,1024]{1,2,0:T(8,128)(2,1)}, bf16[2,128,1024]{1,2,0:T(8,128)(2,1)S(1)}, u32[]{:S(2)}, u32[]{:S(2)}) %collective-permute-start) | collective-permute-done | bytes 524320 | tf_op jit(solution)/shard_map/while/body/eval_jaxpr/ppermute | solution.py:14
  55.1 0.9 fusion.90
  56.0 0.9 fusion.89
  57.6 2.0 collective-permute-start
  60.0 8.6 %collective-permute-done = bf16[2,128,1024]{1,2,0:T(8,128)(2,1)S(1)} collective-permute-done((bf16[2,128,1024]{1,2,0:T(8,128)(2,1)}, bf16[2,128,1024]{1,2,0:T(8,128)(2,1)S(1)}, u32[]{:S(2)}, u32[]{:S(2)}) %collective-permute-start) | collective-permute-done | bytes 524320 | tf_op jit(solution)/shard_map/while/body/eval_jaxpr/ppermute | solution.py:14
  70.9 0.9 fusion.90
  71.7 0.9 fusion.89
  73.7 10.6 %collective-permute-done = bf16[2,128,1024]{1,2,0:T(8,128)(2,1)S(1)} collective-permute-done((bf16[2,128,1024]{1,2,0:T(8,128)(2,1)}, bf16[2,128,1024]{1,2,0:T(8,128)(2,1)S(1)}, u32[]{:S(2)}, u32[]{:S(2)}) %collective-permute-start) | collective-permute-done | bytes 524320 | tf_op jit(solution)/shard_map/while/body/eval_jaxpr/ppermute | solution.py:14
  86.6 0.9 fusion.90
  87.5 0.9 fusion.89
  89.5 10.6 %collective-permute-done = bf16[2,128,1024]{1,2,0:T(8,128)(2,1)S(1)} collective-permute-done((bf16[2,128,1024]{1,2,0:T(8,128)(2,1)}, bf16[2,128,1024]{1,2,0:T(8,128)(2,1)S(1)}, u32[]{:S(2)}, u32[]{:S(2)}) %collective-permute-start) | collective-permute-done | bytes 524320 | tf_op jit(solution)/shard_map/while/body/eval_jaxpr/ppermute | solution.py:14
  102.4 0.9 fusion.90
  103.3 0.9 fusion.89
  105.3 10.6 %collective-permute-done = bf16[2,128,1024]{1,2,0:T(8,128)(2,1)S(1)} collective-permute-done((bf16[2,128,1024]{1,2,0:T(8,128)(2,1)}, bf16[2,128,1024]{1,2,0:T(8,128)(2,1)S(1)}, u32[]{:S(2)}, u32[]{:S(2)}) %collective-permute-start) | collective-permute-done | bytes 524320 | tf_op jit(solution)/shard_map/while/body/eval_jaxpr/ppermute | solution.py:14
  118.2 0.9 fusion.90
  121.0 10.6 %collective-permute-done = bf16[2,128,1024]{1,2,0:T(8,128)(2,1)S(1)} collective-permute-done((bf16[2,128,1024]{1,2,0:T(8,128)(2,1)}, bf16[2,128,1024]{1,2,0:T(8,128)(2,1)S(1)}, u32[]{:S(2)}, u32[]{:S(2)}) %collective-permute-start) | collective-permute-done | bytes 524320 | tf_op jit(solution)/shard_map/while/body/eval_jaxpr/ppermute | solution.py:14
  136.8 10.6 %collective-permute-done = bf16[2,128,1024]{1,2,0:T(8,128)(2,1)S(1)} collective-permute-done((bf16[2,128,1024]{1,2,0:T(8,128)(2,1)}, bf16[2,128,1024]{1,2,0:T(8,128)(2,1)S(1)}, u32[]{:S(2)}, u32[]{:S(2)}) %collective-permute-start) | collective-permute-done | bytes 524320 | tf_op jit(solution)/shard_map/while/body/eval_jaxpr/ppermute | solution.py:14
  150.6 0.9 fusion.89
  152.6 10.6 %collective-permute-done = bf16[2,128,1024]{1,2,0:T(8,128)(2,1)S(1)} collective-permute-done((bf16[2,128,1024]{1,2,0:T(8,128)(2,1)}, bf16[2,128,1024]{1,2,0:T(8,128)(2,1)S(1)}, u32[]{:S(2)}, u32[]{:S(2)}) %collective-permute-start) | collective-permute-done | bytes 524320 | tf_op jit(solution)/shard_map/while/body/eval_jaxpr/ppermute | solution.py:14
  165.5 0.9 fusion.90
  168.4 10.6 %collective-permute-done = bf16[2,128,1024]{1,2,0:T(8,128)(2,1)S(1)} collective-permute-done((bf16[2,128,1024]{1,2,0:T(8,128)(2,1)}, bf16[2,128,1024]{1,2,0:T(8,128)(2,1)S(1)}, u32[]{:S(2)}, u32[]{:S(2)}) %collective-permute-start) | collective-permute-done | bytes 524320 | tf_op jit(solution)/shard_map/while/body/eval_jaxpr/ppermute | solution.py:14
  184.1 10.6 %collective-permute-done = bf16[2,128,1024]{1,2,0:T(8,128)(2,1)S(1)} collective-permute-done((bf16[2,128,1024]{1,2,0:T(8,128)(2,1)}, bf16[2,128,1024]{1,2,0:T(8,128)(2,1)S(1)}, u32[]{:S(2)}, u32[]{:S(2)}) %collective-permute-start) | collective-permute-done | bytes 524320 | tf_op jit(solution)/shard_map/while/body/eval_jaxpr/ppermute | solution.py:14
  199.9 10.6 %collective-permute-done = bf16[2,128,1024]{1,2,0:T(8,128)(2,1)S(1)} collective-permute-done((bf16[2,128,1024]{1,2,0:T(8,128)(2,1)}, bf16[2,128,1024]{1,2,0:T(8,128)(2,1)S(1)}, u32[]{:S(2)}, u32[]{:S(2)}) %collective-permute-start) | collective-permute-done | bytes 524320 | tf_op jit(solution)/shard_map/while/body/eval_jaxpr/ppermute | solution.py:14
  215.7 10.6 %collective-permute-done = bf16[2,128,1024]{1,2,0:T(8,128)(2,1)S(1)} collective-permute-done((bf16[2,128,1024]{1,2,0:T(8,128)(2,1)}, bf16[2,128,1024]{1,2,0:T(8,128)(2,1)S(1)}, u32[]{:S(2)}, u32[]{:S(2)}) %collective-permute-start) | collective-permute-done | bytes 524320 | tf_op jit(solution)/shard_map/while/body/eval_jaxpr/ppermute | solution.py:14
  231.5 10.6 %collective-permute-done = bf16[2,128,1024]{1,2,0:T(8,128)(2,1)S(1)} collective-permute-done((bf16[2,128,1024]{1,2,0:T(8,128)(2,1)}, bf16[2,128,1024]{1,2,0:T(8,128)(2,1)S(1)}, u32[]{:S(2)}, u32[]{:S(2)}) %collective-permute-start) | collective-permute-done | bytes 524320 | tf_op jit(solution)/shard_map/while/body/eval_jaxpr/ppermute | solution.py:14
  247.2 10.6 %collective-permute-done = bf16[2,128,1024]{1,2,0:T(8,128)(2,1)S(1)} collective-permute-done((bf16[2,128,1024]{1,2,0:T(8,128)(2,1)}, bf16[2,128,1024]{1,2,0:T(8,128)(2,1)S(1)}, u32[]{:S(2)}, u32[]{:S(2)}) %collective-permute-start) | collective-permute-done | bytes 524320 | tf_op jit(solution)/shard_map/while/body/eval_jaxpr/ppermute | solution.py:14
  261.0 0.9 fusion.89
  263.0 10.6 %collective-permute-done = bf16[2,128,1024]{1,2,0:T(8,128)(2,1)S(1)} collective-permute-done((bf16[2,128,1024]{1,2,0:T(8,128)(2,1)}, bf16[2,128,1024]{1,2,0:T(8,128)(2,1)S(1)}, u32[]{:S(2)}, u32[]{:S(2)}) %collective-permute-start) | collective-permute-done | bytes 524320 | tf_op jit(solution)/shard_map/while/body/eval_jaxpr/ppermute | solution.py:14
  278.8 10.6 %collective-permute-done = bf16[2,128,1024]{1,2,0:T(8,128)(2,1)S(1)} collective-permute-done((bf16[2,128,1024]{1,2,0:T(8,128)(2,1)}, bf16[2,128,1024]{1,2,0:T(8,128)(2,1)S(1)}, u32[]{:S(2)}, u32[]{:S(2)}) %collective-permute-start) | collective-permute-done | bytes 524320 | tf_op jit(solution)/shard_map/while/body/eval_jaxpr/ppermute | solution.py:14
  294.5 10.6 %collective-permute-done = bf16[2,128,1024]{1,2,0:T(8,128)(2,1)S(1)} collective-permute-done((bf16[2,128,1024]{1,2,0:T(8,128)(2,1)}, bf16[2,128,1024]{1,2,0:T(8,128)(2,1)S(1)}, u32[]{:S(2)}, u32[]{:S(2)}) %collective-permute-start) | collective-permute-done | bytes 524320 | tf_op jit(solution)/shard_map/while/body/eval_jaxpr/ppermute | solution.py:14
  310.3 10.6 %collective-permute-done = bf16[2,128,1024]{1,2,0:T(8,128)(2,1)S(1)} collective-permute-done((bf16[2,128,1024]{1,2,0:T(8,128)(2,1)}, bf16[2,128,1024]{1,2,0:T(8,128)(2,1)S(1)}, u32[]{:S(2)}, u32[]{:S(2)}) %collective-permute-start) | collective-permute-done | bytes 524320 | tf_op jit(solution)/shard_map/while/body/eval_jaxpr/ppermute | solution.py:14
  326.1 10.6 %collective-permute-done = bf16[2,128,1024]{1,2,0:T(8,128)(2,1)S(1)} collective-permute-done((bf16[2,128,1024]{1,2,0:T(8,128)(2,1)}, bf16[2,128,1024]{1,2,0:T(8,128)(2,1)S(1)}, u32[]{:S(2)}, u32[]{:S(2)}) %collective-permute-start) | collective-permute-done | bytes 524320 | tf_op jit(solution)/shard_map/while/body/eval_jaxpr/ppermute | solution.py:14
  341.9 10.6 %collective-permute-done = bf16[2,128,1024]{1,2,0:T(8,128)(2,1)S(1)} collective-permute-done((bf16[2,128,1024]{1,2,0:T(8,128)(2,1)}, bf16[2,128,1024]{1,2,0:T(8,128)(2,1)S(1)}, u32[]{:S(2)}, u32[]{:S(2)}) %collective-permute-start) | collective-permute-done | bytes 524320 | tf_op jit(solution)/shard_map/while/body/eval_jaxpr/ppermute | solution.py:14
  354.8 0.9 fusion.90
  357.6 10.6 %collective-permute-done = bf16[2,128,1024]{1,2,0:T(8,128)(2,1)S(1)} collective-permute-done((bf16[2,128,1024]{1,2,0:T(8,128)(2,1)}, bf16[2,128,1024]{1,2,0:T(8,128)(2,1)S(1)}, u32[]{:S(2)}, u32[]{:S(2)}) %collective-permute-start) | collective-permute-done | bytes 524320 | tf_op jit(solution)/shard_map/while/body/eval_jaxpr/ppermute | solution.py:14
  373.4 10.6 %collective-permute-done = bf16[2,128,1024]{1,2,0:T(8,128)(2,1)S(1)} collective-permute-done((bf16[2,128,1024]{1,2,0:T(8,128)(2,1)}, bf16[2,128,1024]{1,2,0:T(8,128)(2,1)S(1)}, u32[]{:S(2)}, u32[]{:S(2)}) %collective-permute-start) | collective-permute-done | bytes 524320 | tf_op jit(solution)/shard_map/while/body/eval_jaxpr/ppermute | solution.py:14
  389.2 10.6 %collective-permute-done = bf16[2,128,1024]{1,2,0:T(8,128)(2,1)S(1)} collective-permute-done((bf16[2,128,1024]{1,2,0:T(8,128)(2,1)}, bf16[2,128,1024]{1,2,0:T(8,128)(2,1)S(1)}, u32[]{:S(2)}, u32[]{:S(2)}) %collective-permute-start) | collective-permute-done | bytes 524320 | tf_op jit(solution)/shard_map/while/body/eval_jaxpr/ppermute | solution.py:14
  404.9 10.6 %collective-permute-done = bf16[2,128,1024]{1,2,0:T(8,128)(2,1)S(1)} collective-permute-done((bf16[2,128,1024]{1,2,0:T(8,128)(2,1)}, bf16[2,128,1024]{1,2,0:T(8,128)(2,1)S(1)}, u32[]{:S(2)}, u32[]{:S(2)}) %collective-permute-start) | collective-permute-done | bytes 524320 | tf_op jit(solution)/shard_map/while/body/eval_jaxpr/ppermute | solution.py:14
  420.7 10.6 %collective-permute-done = bf16[2,128,1024]{1,2,0:T(8,128)(2,1)S(1)} collective-permute-done((bf16[2,128,1024]{1,2,0:T(8,128)(2,1)}, bf16[2,128,1024]{1,2,0:T(8,128)(2,1)S(1)}, u32[]{:S(2)}, u32[]{:S(2)}) %collective-permute-start) | collective-permute-done | bytes 524320 | tf_op jit(solution)/shard_map/while/body/eval_jaxpr/ppermute | solution.py:14
  436.5 10.6 %collective-permute-done = bf16[2,128,1024]{1,2,0:T(8,128)(2,1)S(1)} collective-permute-done((bf16[2,128,1024]{1,2,0:T(8,128)(2,1)}, bf16[2,128,1024]{1,2,0:T(8,128)(2,1)S(1)}, u32[]{:S(2)}, u32[]{:S(2)}) %collective-permute-start) | collective-permute-done | bytes 524320 | tf_op jit(solution)/shard_map/while/body/eval_jaxpr/ppermute | solution.py:14
  450.3 0.9 fusion.89
  452.3 10.6 %collective-permute-done = bf16[2,128,1024]{1,2,0:T(8,128)(2,1)S(1)} collective-permute-done((bf16[2,128,1024]{1,2,0:T(8,128)(2,1)}, bf16[2,128,1024]{1,2,0:T(8,128)(2,1)S(1)}, u32[]{:S(2)}, u32[]{:S(2)}) %collective-permute-start) | collective-permute-done | bytes 524320 | tf_op jit(solution)/shard_map/while/body/eval_jaxpr/ppermute | solution.py:14
  465.2 0.9 fusion.90
  468.0 10.6 %collective-permute-done = bf16[2,128,1024]{1,2,0:T(8,128)(2,1)S(1)} collective-permute-done((bf16[2,128,1024]{1,2,0:T(8,128)(2,1)}, bf16[2,128,1024]{1,2,0:T(8,128)(2,1)S(1)}, u32[]{:S(2)}, u32[]{:S(2)}) %collective-permute-start) | collective-permute-done | bytes 524320 | tf_op jit(solution)/shard_map/while/body/eval_jaxpr/ppermute | solution.py:14
  483.8 10.6 %collective-permute-done = bf16[2,128,1024]{1,2,0:T(8,128)(2,1)S(1)} collective-permute-done((bf16[2,128,1024]{1,2,0:T(8,128)(2,1)}, bf16[2,128,1024]{1,2,0:T(8,128)(2,1)S(1)}, u32[]{:S(2)}, u32[]{:S(2)}) %collective-permute-start) | collective-permute-done | bytes 524320 | tf_op jit(solution)/shard_map/while/body/eval_jaxpr/ppermute | solution.py:14
  499.3 1.5 copy.59
  500.7 1.5 divide_convert_fusion
  502.2 1.1 copy.61
  503.9 1.1 copy.60
  (703 shorter events, 148.8 us)
Async XLA Ops:
  0.6 3.0 copy-start.9
  12.4 3.3 copy-start.13
  15.7 9.5 %collective-permute-start = (bf16[2,128,1024]{1,2,0:T(8,128)(2,1)}, bf16[2,128,1024]{1,2,0:T(8,128)(2,1)S(1)}, u32[]{:S(2)}, u32[]{:S(2)}) collective-permute-start(bf16[2,128,1024]{1,2,0:T(8,128)(2,1)} %get-tuple-element.680), channel_id=1, source_target_pairs={{248,0},{0,8},{8,16},{16,24},{24,32},{32,40},{40,48},{48,56},{56,6... | collective-permute-start | bytes 1572872 | tf_op jit(solution)/shard_map/while/body/eval_jaxpr/ppermute | solution.py:14
  18.7 6.5 %copy-start = (bf16[128,4,5,128]{3,0,2,1:T(8,128)(2,1)S(1)}, bf16[128,4,5,128]{3,0,2,1:T(8,128)(2,1)}, u32[]{:S(2)}) copy-start(bf16[128,4,5,128]{3,0,2,1:T(8,128)(2,1)} %get-tuple-element.705) | copy-start | bytes 1966084 | tf_op jit(solution)/shard_map/while
  30.0 8.8 %collective-permute-start = (bf16[2,128,1024]{1,2,0:T(8,128)(2,1)}, bf16[2,128,1024]{1,2,0:T(8,128)(2,1)S(1)}, u32[]{:S(2)}, u32[]{:S(2)}) collective-permute-start(bf16[2,128,1024]{1,2,0:T(8,128)(2,1)} %get-tuple-element.680), channel_id=1, source_target_pairs={{248,0},{0,8},{8,16},{16,24},{24,32},{32,40},{40,48},{48,56},{56,6... | collective-permute-start | bytes 1572872 | tf_op jit(solution)/shard_map/while/body/eval_jaxpr/ppermute | solution.py:14
  32.4 6.5 %copy-start = (bf16[128,4,5,128]{3,0,2,1:T(8,128)(2,1)S(1)}, bf16[128,4,5,128]{3,0,2,1:T(8,128)(2,1)}, u32[]{:S(2)}) copy-start(bf16[128,4,5,128]{3,0,2,1:T(8,128)(2,1)} %get-tuple-element.705) | copy-start | bytes 1966084 | tf_op jit(solution)/shard_map/while
  43.7 9.1 %collective-permute-start = (bf16[2,128,1024]{1,2,0:T(8,128)(2,1)}, bf16[2,128,1024]{1,2,0:T(8,128)(2,1)S(1)}, u32[]{:S(2)}, u32[]{:S(2)}) collective-permute-start(bf16[2,128,1024]{1,2,0:T(8,128)(2,1)} %get-tuple-element.680), channel_id=1, source_target_pairs={{248,0},{0,8},{8,16},{16,24},{24,32},{32,40},{40,48},{48,56},{56,6... | collective-permute-start | bytes 1572872 | tf_op jit(solution)/shard_map/while/body/eval_jaxpr/ppermute | solution.py:14
  46.0 6.8 %copy-start = (bf16[128,4,5,128]{3,0,2,1:T(8,128)(2,1)S(1)}, bf16[128,4,5,128]{3,0,2,1:T(8,128)(2,1)}, u32[]{:S(2)}) copy-start(bf16[128,4,5,128]{3,0,2,1:T(8,128)(2,1)} %get-tuple-element.705) | copy-start | bytes 1966084 | tf_op jit(solution)/shard_map/while
  57.6 10.9 %collective-permute-start = (bf16[2,128,1024]{1,2,0:T(8,128)(2,1)}, bf16[2,128,1024]{1,2,0:T(8,128)(2,1)S(1)}, u32[]{:S(2)}, u32[]{:S(2)}) collective-permute-start(bf16[2,128,1024]{1,2,0:T(8,128)(2,1)} %get-tuple-element.680), channel_id=1, source_target_pairs={{248,0},{0,8},{8,16},{16,24},{24,32},{32,40},{40,48},{48,56},{56,6... | collective-permute-start | bytes 1572872 | tf_op jit(solution)/shard_map/while/body/eval_jaxpr/ppermute | solution.py:14
  59.7 8.9 %copy-start = (bf16[128,4,5,128]{3,0,2,1:T(8,128)(2,1)S(1)}, bf16[128,4,5,128]{3,0,2,1:T(8,128)(2,1)}, u32[]{:S(2)}) copy-start(bf16[128,4,5,128]{3,0,2,1:T(8,128)(2,1)} %get-tuple-element.705) | copy-start | bytes 1966084 | tf_op jit(solution)/shard_map/while
  73.4 10.9 %collective-permute-start = (bf16[2,128,1024]{1,2,0:T(8,128)(2,1)}, bf16[2,128,1024]{1,2,0:T(8,128)(2,1)S(1)}, u32[]{:S(2)}, u32[]{:S(2)}) collective-permute-start(bf16[2,128,1024]{1,2,0:T(8,128)(2,1)} %get-tuple-element.680), channel_id=1, source_target_pairs={{248,0},{0,8},{8,16},{16,24},{24,32},{32,40},{40,48},{48,56},{56,6... | collective-permute-start | bytes 1572872 | tf_op jit(solution)/shard_map/while/body/eval_jaxpr/ppermute | solution.py:14
  73.4 11.0 %copy-start = (bf16[128,4,5,128]{3,0,2,1:T(8,128)(2,1)S(1)}, bf16[128,4,5,128]{3,0,2,1:T(8,128)(2,1)}, u32[]{:S(2)}) copy-start(bf16[128,4,5,128]{3,0,2,1:T(8,128)(2,1)} %get-tuple-element.705) | copy-start | bytes 1966084 | tf_op jit(solution)/shard_map/while
  89.2 10.9 %collective-permute-start = (bf16[2,128,1024]{1,2,0:T(8,128)(2,1)}, bf16[2,128,1024]{1,2,0:T(8,128)(2,1)S(1)}, u32[]{:S(2)}, u32[]{:S(2)}) collective-permute-start(bf16[2,128,1024]{1,2,0:T(8,128)(2,1)} %get-tuple-element.680), channel_id=1, source_target_pairs={{248,0},{0,8},{8,16},{16,24},{24,32},{32,40},{40,48},{48,56},{56,6... | collective-permute-start | bytes 1572872 | tf_op jit(solution)/shard_map/while/body/eval_jaxpr/ppermute | solution.py:14
  89.2 11.0 %copy-start = (bf16[128,4,5,128]{3,0,2,1:T(8,128)(2,1)S(1)}, bf16[128,4,5,128]{3,0,2,1:T(8,128)(2,1)}, u32[]{:S(2)}) copy-start(bf16[128,4,5,128]{3,0,2,1:T(8,128)(2,1)} %get-tuple-element.705) | copy-start | bytes 1966084 | tf_op jit(solution)/shard_map/while
  105.0 10.9 %collective-permute-start = (bf16[2,128,1024]{1,2,0:T(8,128)(2,1)}, bf16[2,128,1024]{1,2,0:T(8,128)(2,1)S(1)}, u32[]{:S(2)}, u32[]{:S(2)}) collective-permute-start(bf16[2,128,1024]{1,2,0:T(8,128)(2,1)} %get-tuple-element.680), channel_id=1, source_target_pairs={{248,0},{0,8},{8,16},{16,24},{24,32},{32,40},{40,48},{48,56},{56,6... | collective-permute-start | bytes 1572872 | tf_op jit(solution)/shard_map/while/body/eval_jaxpr/ppermute | solution.py:14
  105.0 11.0 %copy-start = (bf16[128,4,5,128]{3,0,2,1:T(8,128)(2,1)S(1)}, bf16[128,4,5,128]{3,0,2,1:T(8,128)(2,1)}, u32[]{:S(2)}) copy-start(bf16[128,4,5,128]{3,0,2,1:T(8,128)(2,1)} %get-tuple-element.705) | copy-start | bytes 1966084 | tf_op jit(solution)/shard_map/while
  120.7 10.9 %collective-permute-start = (bf16[2,128,1024]{1,2,0:T(8,128)(2,1)}, bf16[2,128,1024]{1,2,0:T(8,128)(2,1)S(1)}, u32[]{:S(2)}, u32[]{:S(2)}) collective-permute-start(bf16[2,128,1024]{1,2,0:T(8,128)(2,1)} %get-tuple-element.680), channel_id=1, source_target_pairs={{248,0},{0,8},{8,16},{16,24},{24,32},{32,40},{40,48},{48,56},{56,6... | collective-permute-start | bytes 1572872 | tf_op jit(solution)/shard_map/while/body/eval_jaxpr/ppermute | solution.py:14
  120.7 11.0 %copy-start = (bf16[128,4,5,128]{3,0,2,1:T(8,128)(2,1)S(1)}, bf16[128,4,5,128]{3,0,2,1:T(8,128)(2,1)}, u32[]{:S(2)}) copy-start(bf16[128,4,5,128]{3,0,2,1:T(8,128)(2,1)} %get-tuple-element.705) | copy-start | bytes 1966084 | tf_op jit(solution)/shard_map/while
  136.5 10.9 %collective-permute-start = (bf16[2,128,1024]{1,2,0:T(8,128)(2,1)}, bf16[2,128,1024]{1,2,0:T(8,128)(2,1)S(1)}, u32[]{:S(2)}, u32[]{:S(2)}) collective-permute-start(bf16[2,128,1024]{1,2,0:T(8,128)(2,1)} %get-tuple-element.680), channel_id=1, source_target_pairs={{248,0},{0,8},{8,16},{16,24},{24,32},{32,40},{40,48},{48,56},{56,6... | collective-permute-start | bytes 1572872 | tf_op jit(solution)/shard_map/while/body/eval_jaxpr/ppermute | solution.py:14
  136.5 11.0 %copy-start = (bf16[128,4,5,128]{3,0,2,1:T(8,128)(2,1)S(1)}, bf16[128,4,5,128]{3,0,2,1:T(8,128)(2,1)}, u32[]{:S(2)}) copy-start(bf16[128,4,5,128]{3,0,2,1:T(8,128)(2,1)} %get-tuple-element.705) | copy-start | bytes 1966084 | tf_op jit(solution)/shard_map/while
  152.3 10.9 %collective-permute-start = (bf16[2,128,1024]{1,2,0:T(8,128)(2,1)}, bf16[2,128,1024]{1,2,0:T(8,128)(2,1)S(1)}, u32[]{:S(2)}, u32[]{:S(2)}) collective-permute-start(bf16[2,128,1024]{1,2,0:T(8,128)(2,1)} %get-tuple-element.680), channel_id=1, source_target_pairs={{248,0},{0,8},{8,16},{16,24},{24,32},{32,40},{40,48},{48,56},{56,6... | collective-permute-start | bytes 1572872 | tf_op jit(solution)/shard_map/while/body/eval_jaxpr/ppermute | solution.py:14
  152.3 11.0 %copy-start = (bf16[128,4,5,128]{3,0,2,1:T(8,128)(2,1)S(1)}, bf16[128,4,5,128]{3,0,2,1:T(8,128)(2,1)}, u32[]{:S(2)}) copy-start(bf16[128,4,5,128]{3,0,2,1:T(8,128)(2,1)} %get-tuple-element.705) | copy-start | bytes 1966084 | tf_op jit(solution)/shard_map/while
  168.0 10.9 %collective-permute-start = (bf16[2,128,1024]{1,2,0:T(8,128)(2,1)}, bf16[2,128,1024]{1,2,0:T(8,128)(2,1)S(1)}, u32[]{:S(2)}, u32[]{:S(2)}) collective-permute-start(bf16[2,128,1024]{1,2,0:T(8,128)(2,1)} %get-tuple-element.680), channel_id=1, source_target_pairs={{248,0},{0,8},{8,16},{16,24},{24,32},{32,40},{40,48},{48,56},{56,6... | collective-permute-start | bytes 1572872 | tf_op jit(solution)/shard_map/while/body/eval_jaxpr/ppermute | solution.py:14
  168.1 11.0 %copy-start = (bf16[128,4,5,128]{3,0,2,1:T(8,128)(2,1)S(1)}, bf16[128,4,5,128]{3,0,2,1:T(8,128)(2,1)}, u32[]{:S(2)}) copy-start(bf16[128,4,5,128]{3,0,2,1:T(8,128)(2,1)} %get-tuple-element.705) | copy-start | bytes 1966084 | tf_op jit(solution)/shard_map/while
  183.8 10.9 %collective-permute-start = (bf16[2,128,1024]{1,2,0:T(8,128)(2,1)}, bf16[2,128,1024]{1,2,0:T(8,128)(2,1)S(1)}, u32[]{:S(2)}, u32[]{:S(2)}) collective-permute-start(bf16[2,128,1024]{1,2,0:T(8,128)(2,1)} %get-tuple-element.680), channel_id=1, source_target_pairs={{248,0},{0,8},{8,16},{16,24},{24,32},{32,40},{40,48},{48,56},{56,6... | collective-permute-start | bytes 1572872 | tf_op jit(solution)/shard_map/while/body/eval_jaxpr/ppermute | solution.py:14
  183.8 11.0 %copy-start = (bf16[128,4,5,128]{3,0,2,1:T(8,128)(2,1)S(1)}, bf16[128,4,5,128]{3,0,2,1:T(8,128)(2,1)}, u32[]{:S(2)}) copy-start(bf16[128,4,5,128]{3,0,2,1:T(8,128)(2,1)} %get-tuple-element.705) | copy-start | bytes 1966084 | tf_op jit(solution)/shard_map/while
  199.6 10.9 %collective-permute-start = (bf16[2,128,1024]{1,2,0:T(8,128)(2,1)}, bf16[2,128,1024]{1,2,0:T(8,128)(2,1)S(1)}, u32[]{:S(2)}, u32[]{:S(2)}) collective-permute-start(bf16[2,128,1024]{1,2,0:T(8,128)(2,1)} %get-tuple-element.680), channel_id=1, source_target_pairs={{248,0},{0,8},{8,16},{16,24},{24,32},{32,40},{40,48},{48,56},{56,6... | collective-permute-start | bytes 1572872 | tf_op jit(solution)/shard_map/while/body/eval_jaxpr/ppermute | solution.py:14
  199.6 11.0 %copy-start = (bf16[128,4,5,128]{3,0,2,1:T(8,128)(2,1)S(1)}, bf16[128,4,5,128]{3,0,2,1:T(8,128)(2,1)}, u32[]{:S(2)}) copy-start(bf16[128,4,5,128]{3,0,2,1:T(8,128)(2,1)} %get-tuple-element.705) | copy-start | bytes 1966084 | tf_op jit(solution)/shard_map/while
  215.4 10.9 %collective-permute-start = (bf16[2,128,1024]{1,2,0:T(8,128)(2,1)}, bf16[2,128,1024]{1,2,0:T(8,128)(2,1)S(1)}, u32[]{:S(2)}, u32[]{:S(2)}) collective-permute-start(bf16[2,128,1024]{1,2,0:T(8,128)(2,1)} %get-tuple-element.680), channel_id=1, source_target_pairs={{248,0},{0,8},{8,16},{16,24},{24,32},{32,40},{40,48},{48,56},{56,6... | collective-permute-start | bytes 1572872 | tf_op jit(solution)/shard_map/while/body/eval_jaxpr/ppermute | solution.py:14
  215.4 11.0 %copy-start = (bf16[128,4,5,128]{3,0,2,1:T(8,128)(2,1)S(1)}, bf16[128,4,5,128]{3,0,2,1:T(8,128)(2,1)}, u32[]{:S(2)}) copy-start(bf16[128,4,5,128]{3,0,2,1:T(8,128)(2,1)} %get-tuple-element.705) | copy-start | bytes 1966084 | tf_op jit(solution)/shard_map/while
  231.1 10.9 %collective-permute-start = (bf16[2,128,1024]{1,2,0:T(8,128)(2,1)}, bf16[2,128,1024]{1,2,0:T(8,128)(2,1)S(1)}, u32[]{:S(2)}, u32[]{:S(2)}) collective-permute-start(bf16[2,128,1024]{1,2,0:T(8,128)(2,1)} %get-tuple-element.680), channel_id=1, source_target_pairs={{248,0},{0,8},{8,16},{16,24},{24,32},{32,40},{40,48},{48,56},{56,6... | collective-permute-start | bytes 1572872 | tf_op jit(solution)/shard_map/while/body/eval_jaxpr/ppermute | solution.py:14
  231.1 11.0 %copy-start = (bf16[128,4,5,128]{3,0,2,1:T(8,128)(2,1)S(1)}, bf16[128,4,5,128]{3,0,2,1:T(8,128)(2,1)}, u32[]{:S(2)}) copy-start(bf16[128,4,5,128]{3,0,2,1:T(8,128)(2,1)} %get-tuple-element.705) | copy-start | bytes 1966084 | tf_op jit(solution)/shard_map/while
  246.9 10.9 %collective-permute-start = (bf16[2,128,1024]{1,2,0:T(8,128)(2,1)}, bf16[2,128,1024]{1,2,0:T(8,128)(2,1)S(1)}, u32[]{:S(2)}, u32[]{:S(2)}) collective-permute-start(bf16[2,128,1024]{1,2,0:T(8,128)(2,1)} %get-tuple-element.680), channel_id=1, source_target_pairs={{248,0},{0,8},{8,16},{16,24},{24,32},{32,40},{40,48},{48,56},{56,6... | collective-permute-start | bytes 1572872 | tf_op jit(solution)/shard_map/while/body/eval_jaxpr/ppermute | solution.py:14
  246.9 11.0 %copy-start = (bf16[128,4,5,128]{3,0,2,1:T(8,128)(2,1)S(1)}, bf16[128,4,5,128]{3,0,2,1:T(8,128)(2,1)}, u32[]{:S(2)}) copy-start(bf16[128,4,5,128]{3,0,2,1:T(8,128)(2,1)} %get-tuple-element.705) | copy-start | bytes 1966084 | tf_op jit(solution)/shard_map/while
  262.7 10.9 %collective-permute-start = (bf16[2,128,1024]{1,2,0:T(8,128)(2,1)}, bf16[2,128,1024]{1,2,0:T(8,128)(2,1)S(1)}, u32[]{:S(2)}, u32[]{:S(2)}) collective-permute-start(bf16[2,128,1024]{1,2,0:T(8,128)(2,1)} %get-tuple-element.680), channel_id=1, source_target_pairs={{248,0},{0,8},{8,16},{16,24},{24,32},{32,40},{40,48},{48,56},{56,6... | collective-permute-start | bytes 1572872 | tf_op jit(solution)/shard_map/while/body/eval_jaxpr/ppermute | solution.py:14
  262.7 11.0 %copy-start = (bf16[128,4,5,128]{3,0,2,1:T(8,128)(2,1)S(1)}, bf16[128,4,5,128]{3,0,2,1:T(8,128)(2,1)}, u32[]{:S(2)}) copy-start(bf16[128,4,5,128]{3,0,2,1:T(8,128)(2,1)} %get-tuple-element.705) | copy-start | bytes 1966084 | tf_op jit(solution)/shard_map/while
  278.5 10.9 %collective-permute-start = (bf16[2,128,1024]{1,2,0:T(8,128)(2,1)}, bf16[2,128,1024]{1,2,0:T(8,128)(2,1)S(1)}, u32[]{:S(2)}, u32[]{:S(2)}) collective-permute-start(bf16[2,128,1024]{1,2,0:T(8,128)(2,1)} %get-tuple-element.680), channel_id=1, source_target_pairs={{248,0},{0,8},{8,16},{16,24},{24,32},{32,40},{40,48},{48,56},{56,6... | collective-permute-start | bytes 1572872 | tf_op jit(solution)/shard_map/while/body/eval_jaxpr/ppermute | solution.py:14
  278.5 11.0 %copy-start = (bf16[128,4,5,128]{3,0,2,1:T(8,128)(2,1)S(1)}, bf16[128,4,5,128]{3,0,2,1:T(8,128)(2,1)}, u32[]{:S(2)}) copy-start(bf16[128,4,5,128]{3,0,2,1:T(8,128)(2,1)} %get-tuple-element.705) | copy-start | bytes 1966084 | tf_op jit(solution)/shard_map/while
  294.2 10.9 %collective-permute-start = (bf16[2,128,1024]{1,2,0:T(8,128)(2,1)}, bf16[2,128,1024]{1,2,0:T(8,128)(2,1)S(1)}, u32[]{:S(2)}, u32[]{:S(2)}) collective-permute-start(bf16[2,128,1024]{1,2,0:T(8,128)(2,1)} %get-tuple-element.680), channel_id=1, source_target_pairs={{248,0},{0,8},{8,16},{16,24},{24,32},{32,40},{40,48},{48,56},{56,6... | collective-permute-start | bytes 1572872 | tf_op jit(solution)/shard_map/while/body/eval_jaxpr/ppermute | solution.py:14
  294.2 11.0 %copy-start = (bf16[128,4,5,128]{3,0,2,1:T(8,128)(2,1)S(1)}, bf16[128,4,5,128]{3,0,2,1:T(8,128)(2,1)}, u32[]{:S(2)}) copy-start(bf16[128,4,5,128]{3,0,2,1:T(8,128)(2,1)} %get-tuple-element.705) | copy-start | bytes 1966084 | tf_op jit(solution)/shard_map/while
  310.0 10.9 %collective-permute-start = (bf16[2,128,1024]{1,2,0:T(8,128)(2,1)}, bf16[2,128,1024]{1,2,0:T(8,128)(2,1)S(1)}, u32[]{:S(2)}, u32[]{:S(2)}) collective-permute-start(bf16[2,128,1024]{1,2,0:T(8,128)(2,1)} %get-tuple-element.680), channel_id=1, source_target_pairs={{248,0},{0,8},{8,16},{16,24},{24,32},{32,40},{40,48},{48,56},{56,6... | collective-permute-start | bytes 1572872 | tf_op jit(solution)/shard_map/while/body/eval_jaxpr/ppermute | solution.py:14
  310.0 11.0 %copy-start = (bf16[128,4,5,128]{3,0,2,1:T(8,128)(2,1)S(1)}, bf16[128,4,5,128]{3,0,2,1:T(8,128)(2,1)}, u32[]{:S(2)}) copy-start(bf16[128,4,5,128]{3,0,2,1:T(8,128)(2,1)} %get-tuple-element.705) | copy-start | bytes 1966084 | tf_op jit(solution)/shard_map/while
  325.8 10.9 %collective-permute-start = (bf16[2,128,1024]{1,2,0:T(8,128)(2,1)}, bf16[2,128,1024]{1,2,0:T(8,128)(2,1)S(1)}, u32[]{:S(2)}, u32[]{:S(2)}) collective-permute-start(bf16[2,128,1024]{1,2,0:T(8,128)(2,1)} %get-tuple-element.680), channel_id=1, source_target_pairs={{248,0},{0,8},{8,16},{16,24},{24,32},{32,40},{40,48},{48,56},{56,6... | collective-permute-start | bytes 1572872 | tf_op jit(solution)/shard_map/while/body/eval_jaxpr/ppermute | solution.py:14
  325.8 11.0 %copy-start = (bf16[128,4,5,128]{3,0,2,1:T(8,128)(2,1)S(1)}, bf16[128,4,5,128]{3,0,2,1:T(8,128)(2,1)}, u32[]{:S(2)}) copy-start(bf16[128,4,5,128]{3,0,2,1:T(8,128)(2,1)} %get-tuple-element.705) | copy-start | bytes 1966084 | tf_op jit(solution)/shard_map/while
  341.5 10.9 %collective-permute-start = (bf16[2,128,1024]{1,2,0:T(8,128)(2,1)}, bf16[2,128,1024]{1,2,0:T(8,128)(2,1)S(1)}, u32[]{:S(2)}, u32[]{:S(2)}) collective-permute-start(bf16[2,128,1024]{1,2,0:T(8,128)(2,1)} %get-tuple-element.680), channel_id=1, source_target_pairs={{248,0},{0,8},{8,16},{16,24},{24,32},{32,40},{40,48},{48,56},{56,6... | collective-permute-start | bytes 1572872 | tf_op jit(solution)/shard_map/while/body/eval_jaxpr/ppermute | solution.py:14
  341.5 11.0 %copy-start = (bf16[128,4,5,128]{3,0,2,1:T(8,128)(2,1)S(1)}, bf16[128,4,5,128]{3,0,2,1:T(8,128)(2,1)}, u32[]{:S(2)}) copy-start(bf16[128,4,5,128]{3,0,2,1:T(8,128)(2,1)} %get-tuple-element.705) | copy-start | bytes 1966084 | tf_op jit(solution)/shard_map/while
  357.3 10.9 %collective-permute-start = (bf16[2,128,1024]{1,2,0:T(8,128)(2,1)}, bf16[2,128,1024]{1,2,0:T(8,128)(2,1)S(1)}, u32[]{:S(2)}, u32[]{:S(2)}) collective-permute-start(bf16[2,128,1024]{1,2,0:T(8,128)(2,1)} %get-tuple-element.680), channel_id=1, source_target_pairs={{248,0},{0,8},{8,16},{16,24},{24,32},{32,40},{40,48},{48,56},{56,6... | collective-permute-start | bytes 1572872 | tf_op jit(solution)/shard_map/while/body/eval_jaxpr/ppermute | solution.py:14
  357.3 11.0 %copy-start = (bf16[128,4,5,128]{3,0,2,1:T(8,128)(2,1)S(1)}, bf16[128,4,5,128]{3,0,2,1:T(8,128)(2,1)}, u32[]{:S(2)}) copy-start(bf16[128,4,5,128]{3,0,2,1:T(8,128)(2,1)} %get-tuple-element.705) | copy-start | bytes 1966084 | tf_op jit(solution)/shard_map/while
  373.1 10.9 %collective-permute-start = (bf16[2,128,1024]{1,2,0:T(8,128)(2,1)}, bf16[2,128,1024]{1,2,0:T(8,128)(2,1)S(1)}, u32[]{:S(2)}, u32[]{:S(2)}) collective-permute-start(bf16[2,128,1024]{1,2,0:T(8,128)(2,1)} %get-tuple-element.680), channel_id=1, source_target_pairs={{248,0},{0,8},{8,16},{16,24},{24,32},{32,40},{40,48},{48,56},{56,6... | collective-permute-start | bytes 1572872 | tf_op jit(solution)/shard_map/while/body/eval_jaxpr/ppermute | solution.py:14
  373.1 11.0 %copy-start = (bf16[128,4,5,128]{3,0,2,1:T(8,128)(2,1)S(1)}, bf16[128,4,5,128]{3,0,2,1:T(8,128)(2,1)}, u32[]{:S(2)}) copy-start(bf16[128,4,5,128]{3,0,2,1:T(8,128)(2,1)} %get-tuple-element.705) | copy-start | bytes 1966084 | tf_op jit(solution)/shard_map/while
  388.9 10.9 %collective-permute-start = (bf16[2,128,1024]{1,2,0:T(8,128)(2,1)}, bf16[2,128,1024]{1,2,0:T(8,128)(2,1)S(1)}, u32[]{:S(2)}, u32[]{:S(2)}) collective-permute-start(bf16[2,128,1024]{1,2,0:T(8,128)(2,1)} %get-tuple-element.680), channel_id=1, source_target_pairs={{248,0},{0,8},{8,16},{16,24},{24,32},{32,40},{40,48},{48,56},{56,6... | collective-permute-start | bytes 1572872 | tf_op jit(solution)/shard_map/while/body/eval_jaxpr/ppermute | solution.py:14
  388.9 11.0 %copy-start = (bf16[128,4,5,128]{3,0,2,1:T(8,128)(2,1)S(1)}, bf16[128,4,5,128]{3,0,2,1:T(8,128)(2,1)}, u32[]{:S(2)}) copy-start(bf16[128,4,5,128]{3,0,2,1:T(8,128)(2,1)} %get-tuple-element.705) | copy-start | bytes 1966084 | tf_op jit(solution)/shard_map/while
  404.6 10.9 %collective-permute-start = (bf16[2,128,1024]{1,2,0:T(8,128)(2,1)}, bf16[2,128,1024]{1,2,0:T(8,128)(2,1)S(1)}, u32[]{:S(2)}, u32[]{:S(2)}) collective-permute-start(bf16[2,128,1024]{1,2,0:T(8,128)(2,1)} %get-tuple-element.680), channel_id=1, source_target_pairs={{248,0},{0,8},{8,16},{16,24},{24,32},{32,40},{40,48},{48,56},{56,6... | collective-permute-start | bytes 1572872 | tf_op jit(solution)/shard_map/while/body/eval_jaxpr/ppermute | solution.py:14
  404.6 11.0 %copy-start = (bf16[128,4,5,128]{3,0,2,1:T(8,128)(2,1)S(1)}, bf16[128,4,5,128]{3,0,2,1:T(8,128)(2,1)}, u32[]{:S(2)}) copy-start(bf16[128,4,5,128]{3,0,2,1:T(8,128)(2,1)} %get-tuple-element.705) | copy-start | bytes 1966084 | tf_op jit(solution)/shard_map/while
  420.4 10.9 %collective-permute-start = (bf16[2,128,1024]{1,2,0:T(8,128)(2,1)}, bf16[2,128,1024]{1,2,0:T(8,128)(2,1)S(1)}, u32[]{:S(2)}, u32[]{:S(2)}) collective-permute-start(bf16[2,128,1024]{1,2,0:T(8,128)(2,1)} %get-tuple-element.680), channel_id=1, source_target_pairs={{248,0},{0,8},{8,16},{16,24},{24,32},{32,40},{40,48},{48,56},{56,6... | collective-permute-start | bytes 1572872 | tf_op jit(solution)/shard_map/while/body/eval_jaxpr/ppermute | solution.py:14
  420.4 11.0 %copy-start = (bf16[128,4,5,128]{3,0,2,1:T(8,128)(2,1)S(1)}, bf16[128,4,5,128]{3,0,2,1:T(8,128)(2,1)}, u32[]{:S(2)}) copy-start(bf16[128,4,5,128]{3,0,2,1:T(8,128)(2,1)} %get-tuple-element.705) | copy-start | bytes 1966084 | tf_op jit(solution)/shard_map/while
  436.2 10.9 %collective-permute-start = (bf16[2,128,1024]{1,2,0:T(8,128)(2,1)}, bf16[2,128,1024]{1,2,0:T(8,128)(2,1)S(1)}, u32[]{:S(2)}, u32[]{:S(2)}) collective-permute-start(bf16[2,128,1024]{1,2,0:T(8,128)(2,1)} %get-tuple-element.680), channel_id=1, source_target_pairs={{248,0},{0,8},{8,16},{16,24},{24,32},{32,40},{40,48},{48,56},{56,6... | collective-permute-start | bytes 1572872 | tf_op jit(solution)/shard_map/while/body/eval_jaxpr/ppermute | solution.py:14
  436.2 11.0 %copy-start = (bf16[128,4,5,128]{3,0,2,1:T(8,128)(2,1)S(1)}, bf16[128,4,5,128]{3,0,2,1:T(8,128)(2,1)}, u32[]{:S(2)}) copy-start(bf16[128,4,5,128]{3,0,2,1:T(8,128)(2,1)} %get-tuple-element.705) | copy-start | bytes 1966084 | tf_op jit(solution)/shard_map/while
  452.0 10.9 %collective-permute-start = (bf16[2,128,1024]{1,2,0:T(8,128)(2,1)}, bf16[2,128,1024]{1,2,0:T(8,128)(2,1)S(1)}, u32[]{:S(2)}, u32[]{:S(2)}) collective-permute-start(bf16[2,128,1024]{1,2,0:T(8,128)(2,1)} %get-tuple-element.680), channel_id=1, source_target_pairs={{248,0},{0,8},{8,16},{16,24},{24,32},{32,40},{40,48},{48,56},{56,6... | collective-permute-start | bytes 1572872 | tf_op jit(solution)/shard_map/while/body/eval_jaxpr/ppermute | solution.py:14
  452.0 11.0 %copy-start = (bf16[128,4,5,128]{3,0,2,1:T(8,128)(2,1)S(1)}, bf16[128,4,5,128]{3,0,2,1:T(8,128)(2,1)}, u32[]{:S(2)}) copy-start(bf16[128,4,5,128]{3,0,2,1:T(8,128)(2,1)} %get-tuple-element.705) | copy-start | bytes 1966084 | tf_op jit(solution)/shard_map/while
  467.7 10.9 %collective-permute-start = (bf16[2,128,1024]{1,2,0:T(8,128)(2,1)}, bf16[2,128,1024]{1,2,0:T(8,128)(2,1)S(1)}, u32[]{:S(2)}, u32[]{:S(2)}) collective-permute-start(bf16[2,128,1024]{1,2,0:T(8,128)(2,1)} %get-tuple-element.680), channel_id=1, source_target_pairs={{248,0},{0,8},{8,16},{16,24},{24,32},{32,40},{40,48},{48,56},{56,6... | collective-permute-start | bytes 1572872 | tf_op jit(solution)/shard_map/while/body/eval_jaxpr/ppermute | solution.py:14
  467.7 11.0 %copy-start = (bf16[128,4,5,128]{3,0,2,1:T(8,128)(2,1)S(1)}, bf16[128,4,5,128]{3,0,2,1:T(8,128)(2,1)}, u32[]{:S(2)}) copy-start(bf16[128,4,5,128]{3,0,2,1:T(8,128)(2,1)} %get-tuple-element.705) | copy-start | bytes 1966084 | tf_op jit(solution)/shard_map/while
  483.5 10.9 %collective-permute-start = (bf16[2,128,1024]{1,2,0:T(8,128)(2,1)}, bf16[2,128,1024]{1,2,0:T(8,128)(2,1)S(1)}, u32[]{:S(2)}, u32[]{:S(2)}) collective-permute-start(bf16[2,128,1024]{1,2,0:T(8,128)(2,1)} %get-tuple-element.680), channel_id=1, source_target_pairs={{248,0},{0,8},{8,16},{16,24},{24,32},{32,40},{40,48},{48,56},{56,6... | collective-permute-start | bytes 1572872 | tf_op jit(solution)/shard_map/while/body/eval_jaxpr/ppermute | solution.py:14
  483.5 11.0 %copy-start = (bf16[128,4,5,128]{3,0,2,1:T(8,128)(2,1)S(1)}, bf16[128,4,5,128]{3,0,2,1:T(8,128)(2,1)}, u32[]{:S(2)}) copy-start(bf16[128,4,5,128]{3,0,2,1:T(8,128)(2,1)} %get-tuple-element.705) | copy-start | bytes 1966084 | tf_op jit(solution)/shard_map/while
  (41 other events, 47.2 us)
where the time goes:
time: 515 us; the launch traced here: 505 us
  waiting for transfers between devices  314 us (61%)
  matrix products  86.7 us (17%)
  local copies, waits for them, and re-layouts  58.3 us (11%)
  other arithmetic  32.1 us (6%)
  starting transfers between devices  9.89 us (2%)
    ppermute x31, waiting for transfers between devices, passed_along(): return lax.ppermute(block, axis, route)  314 us
    dot_general x64, matrix products, update(): jnp.einsum('kgts,skd->tkgd', weights.astype(jnp.bfloat16), value_rows, pr...  55 us
    while x217, local copies, waits for them, and re-layouts  44.8 us
    dot_general x64, matrix products, update(): jnp.einsum('tkgd,skd->kgts', queries[model], key_rows, preferred_element_...  31.7 us
    reduce_sum x32, other arithmetic, update(): totals = totals * shrink + jnp.sum(weights, axis=-1)  17.3 us
  transfers between devices with their start and end apart: 31, of which 31 were waited for; matrix products, arithmetic and copies ran while one was open for 2% of the time, Pallas kernels for 0%

commit v1 on v0

v1 whole, which is shorter than its diff:
```python
import functools
import math

import jax
import jax.numpy as jnp
from jax import lax
from jax.experimental import pallas as pl
from jax.experimental.pallas import tpu as pltpu
from jax.sharding import PartitionSpec as P

HK, GROUP, HD, TOK = 4, 5, 128, 128
NZ, NBLK, SPAN = 8, 32, 17
ROWS, KEYS = GROUP * TOK, SPAN * TOK
NDOC = 8
SCALE = math.log2(math.e) / math.sqrt(HD)
BIG = 131072.0
NSIG = 2 * HK
BF, F32 = jnp.bfloat16, jnp.float32
PROLOGUE = (0, 10, 20, 30, 1, 11, 21, 31, 2, 12, 22, 32, 3, 40, 13, 23, 50, 33, 4, 60)
BEFORE_S = {1: (41, 14, 24), 2: (51, 70, 34), 3: (42,), 4: (71, 62, 43, 53, 72, 63, 44, 54), 6: (74,)}
BEFORE_P = {2: (61,), 3: (52,), 4: (73, 64)}


def kernel(n_ctx, qp_ref, kvp_ref, qr_ref, kvr_ref, doc_ref, span_ref, o_ref, *scratch):
    kvb = scratch[:NSIG]
    (qbuf, kaug, vaug, pbuf, qa, abias, elog, obuf, inv,
     lk, lq, yr, ys, yqr, yqs, zr, zs, cr, cs, orecv, osend, olocal) = scratch[NSIG:]
    me = lax.axis_index("ctx")
    y, z, c = me // (2 * NZ), (me // 2) % NZ, me % 2

    def dev(yy, zz, cc):
        return {"ctx": (yy * NZ + zz) * 2 + cc}

    mesh_id = pl.DeviceIdType.MESH
    peer_y, peer_c = dev(1 - y, z, c), dev(y, z, 1 - c)
    up, down = dev(y, (z + 1) % NZ, c), dev(y, (z + NZ - 1) % NZ, c)

    def remote(src, dst, ssem, rsem, to):
        return pltpu.make_async_remote_copy(
            src_ref=src, dst_ref=dst, send_sem=ssem, recv_sem=rsem, device_id=to, device_id_type=mesh_id)

    def slot(zz):
        return c * 2 * NZ + zz * 2

    barrier = pltpu.get_barrier_semaphore()
    for to in (peer_y, peer_c, up, down):
        pl.semaphore_signal(barrier, inc=1, device_id=to, device_id_type=mesh_id)

    def kv_cols(sig):
        return pl.ds((sig % 2) * HK * HD + (sig // 2) * HD, HD)

    def local_copies(kv_ref, q_ref):
        for sig in range(NSIG):
            pltpu.make_async_copy(kv_ref.at[:, kv_cols(sig)], kvb[sig].at[slot(z) + y], lk.at[sig]).start()
        pltpu.make_async_copy(q_ref, qbuf.at[1], lq).start()

    def peer_copies(kv_ref, q_ref):
        for sig in range(NSIG):
            remote(kv_ref.at[:, kv_cols(sig)], kvb[sig].at[slot(z) + y], ys, yr.at[sig], peer_y).start()
        for j in range(HK):
            cols = pl.ds(j * GROUP * HD, GROUP * HD)
            remote(q_ref.at[:, cols], qbuf.at[0, :, cols], yqs, yqr.at[j], peer_y).start()

    @pl.when(y == 0)
    def _():
        local_copies(kvp_ref, qp_ref)

    @pl.when(y == 1)
    def _():
        local_copies(kvr_ref, qr_ref)

    pl.semaphore_wait(barrier, 4)

    @pl.when(y == 0)
    def _():
        peer_copies(kvr_ref, qr_ref)

    @pl.when(y == 1)
    def _():
        peer_copies(kvp_ref, qp_ref)

    def tick(sig, d):
        buf = kvb[sig]

        def push(view):
            remote(view, view, cs.at[sig], cr.at[sig], peer_c).start()

        if d == 0:
            mine = buf.at[slot(z) + y]
            pltpu.make_async_copy(mine, mine, lk.at[sig]).wait()
            theirs = buf.at[slot(z) + 1 - y]
            remote(theirs, theirs, ys, yr.at[sig], peer_y).wait_recv()
            view = buf.at[pl.ds(slot(z), 2)]
            for way, to in ((0, up), (1, down)):
                remote(view, view, zs.at[sig], zr.at[sig, 0, way], to).start()
            push(view)
            return
        for way, to in ((0, up), (1, down)):
            first = slot((z + NZ - d) % NZ if way == 0 else (z + d) % NZ)
            view = buf.at[pl.ds(first, 2)] if d < 4 else buf.at[pl.ds(first + way, 1)]
            remote(view, view, zs.at[sig], zr.at[sig, d - 1, way], to).wait_recv()
            if d < 4:
                onward = view if d < 3 else buf.at[pl.ds(first + way, 1)]
                remote(onward, onward, zs.at[sig], zr.at[sig, d, way], to).start()
                push(view)
        if d == 4:
            push(buf.at[pl.ds(slot((z + 4) % NZ), 2)])

    def tables():
        def fill(k, _):
            acc = jnp.int32(0)
            for m in range(NBLK):
                at = ((m // 2) % NZ) * 2 + (m % 2) * 2 * NZ + m // (2 * NZ)
                acc = jnp.where(span_ref[m] == k, jnp.int32(at), acc)
            inv[k] = acc
            return 0

        lax.fori_loop(0, NBLK, fill, 0)
        lane = lax.broadcasted_iota(jnp.int32, (TOK, HD), 1)
        row = lax.broadcasted_iota(jnp.int32, (TOK, HD), 0)
        first = jnp.where(lane == NDOC, -1000000, 0)
        last = jnp.where(lane == NDOC, 0, -1000000)
        end = jnp.int32(0)
        for k in range(NDOC):
            begin = end
            end = end + doc_ref[k]
            first = jnp.where(lane == k, begin, first)
            last = jnp.where(lane == k, end, last)

        def block(r, _):
            pos = row + (r - 16) * TOK
            hit = (pos >= first) & (pos < last)
            elog[r] = jnp.where(hit, 1.0, 0.0).astype(BF)
            return 0

        lax.fori_loop(0, NBLK + 16, block, 0)
        vaug[:, HD:] = jnp.ones((KEYS, HD), BF)
        for b in range(2):
            place = place_of(b)
            for t in range(SPAN):
                kaug[b, t * TOK:(t + 1) * TOK, HD:] = elog[place + t]
            abias[b] = ((elog[place + 16].astype(F32) - 1.0) * BIG).astype(BF)

    def place_of(b):
        source = jnp.where(b == 0, 1 - y, y) * 2 * NZ + z * 2 + c
        return span_ref[source]

    for count, item in enumerate(PROLOGUE):
        if count == 3:
            tables()
        tick(item // 10, item % 10)
    pltpu.make_async_copy(qbuf.at[1], qbuf.at[1], lq).wait()

    def scores(i):
        j, b = i // 2, i % 2
        place = place_of(b)
        for jj in range(HK):
            sig = 2 * jj

            @pl.when(j == jj)
            def _(sig=sig, jj=jj):
                @pl.when(b == 0)
                def _():
                    half = kvb[sig].at[pl.ds((1 - c) * 2 * NZ, 2 * NZ)]
                    remote(half, half, cs.at[sig], cr.at[sig], peer_c).wait_recv()
                    cols = pl.ds(jj * GROUP * HD, GROUP * HD)
                    part = qbuf.at[0, :, cols]
                    remote(part, part, yqs, yqr.at[jj], peer_y).wait_recv()

                for t in range(SPAN):
                    at = inv[jnp.maximum(place - 16 + t, 0)]
                    kaug[b, t * TOK:(t + 1) * TOK, :HD] = kvb[sig][at]

        for g in range(GROUP):
            cols = pl.ds(pl.multiple_of((j * GROUP + g) * HD, HD), HD)
            qa[g * TOK:(g + 1) * TOK, :HD] = qbuf[b, :, cols]
            qa[g * TOK:(g + 1) * TOK, HD:] = abias[b]
        s = lax.dot_general(qa[...], kaug[b], (((1,), (1,)), ((), ())), preferred_element_type=F32)
        causal = lax.broadcasted_iota(jnp.int32, (TOK, TOK), 1) <= lax.broadcasted_iota(jnp.int32, (TOK, TOK), 0)
        keep = i % 3
        for g in range(GROUP):
            sg = s[g * TOK:(g + 1) * TOK]
            diag = jnp.where(causal, sg[:, KEYS - TOK:], -BIG)
            peak = diag
            for t in range(SPAN - 1):
                peak = jnp.maximum(peak, sg[:, t * TOK:(t + 1) * TOK])
            peak = jnp.max(peak, axis=1, keepdims=True) * SCALE
            pbuf[keep, g * TOK:(g + 1) * TOK, :KEYS - TOK] = jnp.exp2(sg[:, :KEYS - TOK] * SCALE - peak).astype(BF)
            pbuf[keep, g * TOK:(g + 1) * TOK, KEYS - TOK:] = jnp.exp2(diag * SCALE - peak).astype(BF)

    def values(i):
        j, b = i // 2, i % 2
        place = place_of(b)
        for jj in range(HK):
            sig = 2 * jj + 1

            @pl.when(j == jj)
            def _(sig=sig):
                @pl.when(b == 0)
                def _():
                    half = kvb[sig].at[pl.ds((1 - c) * 2 * NZ, 2 * NZ)]
                    remote(half, half, cs.at[sig], cr.at[sig], peer_c).wait_recv()

                for t in range(SPAN):
                    at = inv[jnp.maximum(place - 16 + t, 0)]
                    vaug[t * TOK:(t + 1) * TOK, :HD] = kvb[sig][at]

        o = lax.dot_general(pbuf[i % 3], vaug[...], (((1,), (0,)), ((), ())), preferred_element_type=F32)
        o = (o[:, :HD] / o[:, HD:]).astype(BF)
        for g in range(GROUP):
            obuf[i, :, g * HD:(g + 1) * HD] = o[g * TOK:(g + 1) * TOK]
        cols = pl.ds(pl.multiple_of(j * GROUP * HD, GROUP * HD), GROUP * HD)

        @pl.when(b == 0)
        def _():
            remote(obuf.at[i], o_ref.at[y, :, cols], osend, orecv.at[j], peer_y).start()

        @pl.when(b == 1)
        def _():
            pltpu.make_async_copy(obuf.at[i], o_ref.at[y, :, cols], olocal.at[j]).start()

    @pl.loop(0, 10)
    def _(i):
        for k, items in BEFORE_S.items():
            if items:
                @pl.when(i == k)
                def _(items=items):
                    for item in items:
                        tick(item // 10, item % 10)

        @pl.when(i < 8)
        def _():
            scores(i)

        for k, items in BEFORE_P.items():
            if items:
                @pl.when(i == k)
                def _(items=items):
                    for item in items:
                        tick(item // 10, item % 10)

        @pl.when(i >= 2)
        def _():
            values(i - 2)

    for j in range(HK):
        cols = pl.ds(j * GROUP * HD, GROUP * HD)
        part = o_ref.at[1 - y, :, cols]
        remote(part, part, osend, orecv.at[j], peer_y).wait_recv()
        part = o_ref.at[y, :, cols]
        pltpu.make_async_copy(part, part, olocal.at[j]).wait()
    four = obuf.at[pl.ds(0, HK)]
    remote(four, four, osend, orecv.at[0], peer_y).wait_send()
    remote(qbuf.at[0], qbuf.at[0], yqs, yqr.at[0], peer_y).wait_send()
    eight = kvb[0].at[pl.ds(0, NSIG)]
    remote(eight, eight, ys, yr.at[0], peer_y).wait_send()
    for sig in range(NSIG):
        sent = kvb[sig].at[pl.ds(0, 14)]
        remote(sent, sent, zs.at[sig], zr.at[sig, 0, 0], up).wait_send()
        sent = kvb[sig].at[pl.ds(0, 16)]
        remote(sent, sent, cs.at[sig], cr.at[sig], peer_c).wait_send()


def on_device(n_ctx, q_policy, kv_policy, q_ref, kv_ref, doc_lengths, span_order):
    any_spec = pl.BlockSpec(memory_space=pl.ANY)
    smem = pl.BlockSpec(memory_space=pltpu.SMEM)
    dma = pltpu.SemaphoreType.DMA
    out = pl.pallas_call(
        functools.partial(kernel, n_ctx),
        out_shape=jax.ShapeDtypeStruct((2, TOK, HK * GROUP * HD), BF),
        in_specs=[any_spec] * 4 + [smem] * 2,
        out_specs=any_spec,
        scratch_shapes=[pltpu.VMEM((NBLK, TOK, HD), BF)] * NSIG
        + [
            pltpu.VMEM((2, TOK, HK * GROUP * HD), BF),
            pltpu.VMEM((2, KEYS, 2 * HD), BF),
            pltpu.VMEM((KEYS, 2 * HD), BF),
            pltpu.VMEM((3, ROWS, KEYS), BF),
            pltpu.VMEM((ROWS, 2 * HD), BF),
            pltpu.VMEM((2, TOK, HD), BF),
            pltpu.VMEM((NBLK + 16, TOK, HD), BF),
            pltpu.VMEM((2 * HK, TOK, GROUP * HD), BF),
            pltpu.SMEM((NBLK,), jnp.int32),
            dma((NSIG,)), dma, dma((NSIG,)), dma, dma((HK,)), dma,
            dma((NSIG, 4, 2)), dma((NSIG,)), dma((NSIG,)), dma((NSIG,)),
            dma((HK,)), dma, dma((HK,)),
        ],
        compiler_params=pltpu.CompilerParams(
            collective_id=0, has_side_effects=True, vmem_limit_bytes=52 * 2**20),
        cost_estimate=pl.CostEstimate(flops=6_000_000_000, bytes_accessed=4_000_000, transcendentals=12_000_000),
    )(q_policy, kv_policy, q_ref, kv_ref, doc_lengths, span_order)
    return out[0], out[1]


def solution(mesh):
    spec = P(("rep", "ctx"), None)
    return jax.shard_map(
        functools.partial(on_device, mesh.shape["ctx"]), mesh=mesh,
        in_specs=(spec, spec, spec, spec, P("rep"), P("rep")), out_specs=(spec, spec), check_vma=False)
```

time: 515 us -> 79.1 us (0.15); the launches traced: 505 us -> 78.9 us
  waiting for transfers between devices: 314 us -> 0 us
  matrix products: 86.7 us -> 0 us
  Pallas kernels: 0 us -> 70.4 us
  local copies, waits for them, and re-layouts: 58.3 us -> 7.8 us
  other arithmetic: 32.1 us -> 0 us
  starting transfers between devices: 9.89 us -> 0 us
    ppermute x31 -> x0, waiting for transfers between devices: 314 us -> none  [passed_along(): return lax.ppermute(block, axis, route)]
    dot_general x128 -> x0, matrix products: 86.7 us -> none  [the longest x64 55 us: update(): jnp.einsum('kgts,skd->tkgd', weights.astype(jnp.bfloat16), value_rows, pr...]
    pallas_call x0 -> x1, Pallas kernels: none -> 70.4 us  [on_device(): pl.pallas_call(functools.partial(kernel, n_ctx), out_shape=jax.ShapeDtype...]
    while x219 -> x0, local copies, waits for them, and re-layouts: 46.6 us -> none
    reduce_sum x96 -> x0, other arithmetic: 23.7 us -> none  [the longest x32 17.3 us: update(): totals = totals * shrink + jnp.sum(weights, axis=-1)]
    ppermute x31 -> x0, starting transfers between devices: 9.89 us -> none  [passed_along(): return lax.ppermute(block, axis, route)]
  transfers between devices with their start and end apart: 31 -> 0, of which waited for: 31 -> 0; matrix products, arithmetic and copies ran while one was open for 2% -> 0% of each run, Pallas kernels for 0% -> 0%
where the time goes in v1:
time: 79.1 us; the launch traced here: 78.9 us
  Pallas kernels  70.4 us (89%)
  local copies, waits for them, and re-layouts  7.8 us (10%)
    pallas_call x1, Pallas kernels, on_device(): pl.pallas_call(functools.partial(kernel, n_ctx), out_shape=jax.ShapeDtype...  70.4 us
    unnamed x12, local copies, waits for them, and re-layouts  5.38 us
    squeeze x1, local copies, waits for them, and re-layouts, on_device(): return (out[0], out[1])  2.42 us

profile of v1, /device:TPU:1, one launch (start us, length us, event | category | flops | bytes accessed | tf_op | source)
XLA Modules:
  0.0 78.9 jit_solution(17867438007953352753)
XLA Ops:
  0.6 0.0 copy-start
  0.6 1.1 %copy-done = bf16[128,2560]{1,0:T(8,128)(2,1)S(1)} copy-done((bf16[128,2560]{1,0:T(8,128)(2,1)S(1)}, bf16[128,2560]{1,0:T(8,128)(2,1)}, u32[]{:S(2)}) %copy-start) | copy-done | bytes 655384
  1.7 0.0 copy-start.1
  1.7 1.1 %copy-done.1 = bf16[128,2560]{1,0:T(8,128)(2,1)S(1)} copy-done((bf16[128,2560]{1,0:T(8,128)(2,1)S(1)}, bf16[128,2560]{1,0:T(8,128)(2,1)}, u32[]{:S(2)}) %copy-start.1) | copy-done | bytes 655384
  2.8 0.0 copy-start.2
  2.8 0.9 %copy-done.2 = bf16[128,1024]{1,0:T(8,128)(2,1)S(1)} copy-done((bf16[128,1024]{1,0:T(8,128)(2,1)S(1)}, bf16[128,1024]{1,0:T(8,128)(2,1)}, u32[]{:S(2)}) %copy-start.2) | copy-done | bytes 262168
  3.8 0.0 copy-start.3
  3.8 0.9 %copy-done.3 = bf16[128,1024]{1,0:T(8,128)(2,1)S(1)} copy-done((bf16[128,1024]{1,0:T(8,128)(2,1)S(1)}, bf16[128,1024]{1,0:T(8,128)(2,1)}, u32[]{:S(2)}) %copy-start.3) | copy-done | bytes 262168
  4.7 0.0 copy-start.4
  4.7 0.7 copy-done.4
  5.4 0.0 copy-start.5
  5.4 0.7 copy-done.5
  6.0 70.4 %shard_map.77 = bf16[2,128,2560]{2,1,0:T(8,128)(2,1)} custom-call(bf16[128,2560]{1,0:T(8,128)(2,1)S(1)} %copy-done, bf16[128,1024]{1,0:T(8,128)(2,1)S(1)} %copy-done.2, bf16[128,2560]{1,0:T(8,128)(2,1)S(1)} %copy-done.1, bf16[128,1024]{1,0:T(8,128)(2,1)S(1)} %copy-done.3, s32[8]{0:T(128)S(1)} %copy-done.4, s32[32]{0:T(128)S(1)} %copy-done.5), custom_call_target="tpu_custom_call" | custom-call | flops 6000000000 | bytes 4000000 | tf_op jit(solution)/shard_map/pallas_call | solution.py:268
  76.4 2.4 %slice_bitcast_fusion = (bf16[128,2560]{1,0:T(8,128)(2,1)}, bf16[128,2560]{1,0:T(8,128)(2,1)}) fusion(bf16[2,128,2560]{2,1,0:T(8,128)(2,1)} %shard_map.77), kind=kLoop, calls=%fused_computation | loop fusion | bytes 2621440 | tf_op jit(solution)/shard_map/squeeze | solution.py:292
Async XLA Ops:
  0.6 1.1 %copy-start = (bf16[128,2560]{1,0:T(8,128)(2,1)S(1)}, bf16[128,2560]{1,0:T(8,128)(2,1)}, u32[]{:S(2)}) copy-start(bf16[128,2560]{1,0:T(8,128)(2,1)} %qp_ref.1) | copy-start | bytes 1966084
  1.7 1.1 %copy-start.1 = (bf16[128,2560]{1,0:T(8,128)(2,1)S(1)}, bf16[128,2560]{1,0:T(8,128)(2,1)}, u32[]{:S(2)}) copy-start(bf16[128,2560]{1,0:T(8,128)(2,1)} %qr_ref.1) | copy-start | bytes 1966084
  2.8 0.9 %copy-start.2 = (bf16[128,1024]{1,0:T(8,128)(2,1)S(1)}, bf16[128,1024]{1,0:T(8,128)(2,1)}, u32[]{:S(2)}) copy-start(bf16[128,1024]{1,0:T(8,128)(2,1)} %kvp_ref.1) | copy-start | bytes 786436
  3.8 0.9 %copy-start.3 = (bf16[128,1024]{1,0:T(8,128)(2,1)S(1)}, bf16[128,1024]{1,0:T(8,128)(2,1)}, u32[]{:S(2)}) copy-start(bf16[128,1024]{1,0:T(8,128)(2,1)} %kvr_ref.1) | copy-start | bytes 786436
  4.7 0.7 copy-start.4
  5.4 0.7 copy-start.5

commit v2 on v1

--- a/solution.py
+++ b/solution.py
@@ -16,12 +16,12 @@
 BIG = 131072.0
 NSIG = 2 * HK
 BF, F32 = jnp.bfloat16, jnp.float32
-PROLOGUE = (0, 10, 20, 30, 1, 11, 21, 31, 2, 12, 22, 32, 3, 40, 13, 23, 50, 33, 4, 60)
-BEFORE_S = {1: (41, 14, 24), 2: (51, 70, 34), 3: (42,), 4: (71, 62, 43, 53, 72, 63, 44, 54), 6: (74,)}
-BEFORE_P = {2: (61,), 3: (52,), 4: (73, 64)}
-
-
-def kernel(n_ctx, qp_ref, kvp_ref, qr_ref, kvr_ref, doc_ref, span_ref, o_ref, *scratch):
+PROLOGUE = (0, 20, 10, 40, 1, 21, 30, 11, 2, 22, 41, 12, 3, 23, 31, 60, 42, 13, 4, 50, 70, 24)
+BEFORE_S = {1: (32,), 2: (61, 14), 3: (71,), 4: (52,), 5: (53,), 6: (54,), 7: (74,)}
+BEFORE_P = {2: (43, 51), 3: (33, 62, 44), 4: (72, 34, 63), 5: (73, 64)}
+
+
+def kernel(n_ctx, qp_ref, kvp_ref, qr_ref, kvr_ref, doc_ref, span_ref, op_ref, or_ref, *scratch):
     kvb = scratch[:NSIG]
     (qbuf, kaug, vaug, pbuf, qa, abias, elog, obuf, inv,
      lk, lq, yr, ys, yqr, yqs, zr, zs, cr, cs, orecv, osend, olocal) = scratch[NSIG:]
@@ -86,14 +86,18 @@
             remote(view, view, cs.at[sig], cr.at[sig], peer_c).start()
 
         if d == 0:
-            mine = buf.at[slot(z) + y]
+            mine = buf.at[pl.ds(slot(z) + y, 1)]
+            theirs = buf.at[pl.ds(slot(z) + 1 - y, 1)]
+            both = buf.at[pl.ds(slot(z), 2)]
             pltpu.make_async_copy(mine, mine, lk.at[sig]).wait()
-            theirs = buf.at[slot(z) + 1 - y]
+            if sig < 2:
+                for way, to in ((0, up), (1, down)):
+                    remote(mine, mine, zs.at[sig], zr.at[sig, 0, way], to).start()
             remote(theirs, theirs, ys, yr.at[sig], peer_y).wait_recv()
-            view = buf.at[pl.ds(slot(z), 2)]
+            rest = theirs if sig < 2 else both
             for way, to in ((0, up), (1, down)):
-                remote(view, view, zs.at[sig], zr.at[sig, 0, way], to).start()
-            push(view)
+                remote(rest, rest, zs.at[sig], zr.at[sig, 0, way], to).start()
+            push(both)
             return
         for way, to in ((0, up), (1, down)):
             first = slot((z + NZ - d) % NZ if way == 0 else (z + d) % NZ)
@@ -213,11 +217,17 @@
 
         @pl.when(b == 0)
         def _():
-            remote(obuf.at[i], o_ref.at[y, :, cols], osend, orecv.at[j], peer_y).start()
+            for m, o_ref in enumerate((op_ref, or_ref)):
+                @pl.when(y == m)
+                def _(o_ref=o_ref):
+                    remote(obuf.at[i], o_ref.at[:, cols], osend, orecv.at[j], peer_y).start()
 
         @pl.when(b == 1)
         def _():
-            pltpu.make_async_copy(obuf.at[i], o_ref.at[y, :, cols], olocal.at[j]).start()
+            for m, o_ref in enumerate((op_ref, or_ref)):
+                @pl.when(y == m)
+                def _(o_ref=o_ref):
+                    pltpu.make_async_copy(obuf.at[i], o_ref.at[:, cols], olocal.at[j]).start()
 
     @pl.loop(0, 10)
     def _(i):
@@ -244,10 +254,8 @@
             values(i - 2)
 
     for j in range(HK):
-        cols = pl.ds(j * GROUP * HD, GROUP * HD)
-        part = o_ref.at[1 - y, :, cols]
+        part = obuf.at[j]
         remote(part, part, osend, orecv.at[j], peer_y).wait_recv()
-        part = o_ref.at[y, :, cols]
         pltpu.make_async_copy(part, part, olocal.at[j]).wait()
     four = obuf.at[pl.ds(0, HK)]
     remote(four, four, osend, orecv.at[0], peer_y).wait_send()
@@ -262,14 +270,14 @@
 
 
 def on_device(n_ctx, q_policy, kv_policy, q_ref, kv_ref, doc_lengths, span_order):
-    any_spec = pl.BlockSpec(memory_space=pl.ANY)
+    hbm = pl.BlockSpec(memory_space=pltpu.HBM)
     smem = pl.BlockSpec(memory_space=pltpu.SMEM)
     dma = pltpu.SemaphoreType.DMA
     out = pl.pallas_call(
         functools.partial(kernel, n_ctx),
-        out_shape=jax.ShapeDtypeStruct((2, TOK, HK * GROUP * HD), BF),
-        in_specs=[any_spec] * 4 + [smem] * 2,
-        out_specs=any_spec,
+        out_shape=[jax.ShapeDtypeStruct((TOK, HK * GROUP * HD), BF)] * 2,
+        in_specs=[hbm] * 4 + [smem] * 2,
+        out_specs=[hbm] * 2,
         scratch_shapes=[pltpu.VMEM((NBLK, TOK, HD), BF)] * NSIG
         + [
             pltpu.VMEM((2, TOK, HK * GROUP * HD), BF),
@@ -286,10 +294,10 @@
             dma((HK,)), dma, dma((HK,)),
         ],
         compiler_params=pltpu.CompilerParams(
-            collective_id=0, has_side_effects=True, vmem_limit_bytes=52 * 2**20),
+            collective_id=0, has_side_effects=True, vmem_limit_bytes=63 * 2**20),
         cost_estimate=pl.CostEstimate(flops=6_000_000_000, bytes_accessed=4_000_000, transcendentals=12_000_000),
     )(q_policy, kv_policy, q_ref, kv_ref, doc_lengths, span_order)
-    return out[0], out[1]
+    return tuple(out)
 
 
 def solution(mesh):

time: 79.1 us -> 69.3 us (0.88)
  local copies, waits for them, and re-layouts: 7.8 us -> 2.87 us
  Pallas kernels: 70.4 us -> 65.7 us
    pallas_call x1, Pallas kernels: 70.4 us -> 65.7 us  [on_device(): pl.pallas_call(functools.partial(kernel, n_ctx), out_shape=[jax.ShapeDtyp...]
    unnamed x12 -> x4, local copies, waits for them, and re-layouts: 5.38 us -> 2.87 us
    squeeze x1 -> x0, local copies, waits for them, and re-layouts: 2.42 us -> none  [on_device(): return (out[0], out[1])]
where the time goes in v2:
time: 69.3 us; the launch traced here: 69.2 us
  Pallas kernels  65.7 us (95%)
  local copies, waits for them, and re-layouts  2.87 us (4%)
    pallas_call x1, Pallas kernels, on_device(): pl.pallas_call(functools.partial(kernel, n_ctx), out_shape=[jax.ShapeDtyp...  65.7 us
    unnamed x4, local copies, waits for them, and re-layouts  2.87 us

profile of v2, /device:TPU:1, one launch (start us, length us, event | category | flops | bytes accessed | tf_op | source)
XLA Modules:
  0.0 69.2 jit_solution(17208228028052517537)
XLA Ops:
  0.6 65.7 %shard_map.77 = (bf16[128,2560]{1,0:T(8,128)(2,1)}, bf16[128,2560]{1,0:T(8,128)(2,1)}) custom-call(bf16[128,2560]{1,0:T(8,128)(2,1)} %qp_ref.1, bf16[128,1024]{1,0:T(8,128)(2,1)} %kvp_ref.1, bf16[128,2560]{1,0:T(8,128)(2,1)} %qr_ref.1, bf16[128,1024]{1,0:T(8,128)(2,1)} %kvr_ref.1, s32[8]{0:T(128)} %doc_ref.1, s32[32]{0:T(128)} %span_ref.1), custom_call_target="tpu_custom_call" | custom-call | flops 6000000000 | bytes 4000000 | tf_op jit(solution)/shard_map/pallas_call | solution.py:276
  66.3 0.0 copy-start
  66.3 2.0 %copy.10 = bf16[128,2560]{1,0:T(8,128)(2,1)} copy(bf16[128,2560]{1,0:T(8,128)(2,1)} %get-tuple-element.4) | data formatting | bytes 1310720
  68.4 0.0 copy-done
  68.4 0.8 %copy.11 = bf16[128,2560]{1,0:T(8,128)(2,1)} copy(bf16[128,2560]{1,0:T(8,128)(2,1)S(1)} %copy-done) | data formatting | bytes 1310720
Async XLA Ops:
  66.3 2.0 %copy-start = (bf16[128,2560]{1,0:T(8,128)(2,1)S(1)}, bf16[128,2560]{1,0:T(8,128)(2,1)}, u32[]{:S(2)}) copy-start(bf16[128,2560]{1,0:T(8,128)(2,1)} %get-tuple-element.5) | copy-start | bytes 1966084

commit v3 on v2

--- a/solution.py
+++ b/solution.py
@@ -16,9 +16,8 @@
 BIG = 131072.0
 NSIG = 2 * HK
 BF, F32 = jnp.bfloat16, jnp.float32
-PROLOGUE = (0, 20, 10, 40, 1, 21, 30, 11, 2, 22, 41, 12, 3, 23, 31, 60, 42, 13, 4, 50, 70, 24)
-BEFORE_S = {1: (32,), 2: (61, 14), 3: (71,), 4: (52,), 5: (53,), 6: (54,), 7: (74,)}
-BEFORE_P = {2: (43, 51), 3: (33, 62, 44), 4: (72, 34, 63), 5: (73, 64)}
+PROLOGUE = (0, 10, 20, 30, 1, 11, 21, 40, 2, 31, 12, 22, 3, 50, 13, 41, 23, 4, 60, 32)
+BEFORE = {1: (51, 42, 14), 2: (70,), 3: (33, 24, 61), 4: (52,), 5: (43, 71, 34), 6: (62,), 7: (44, 53), 8: (72,), 9: (63, 54), 10: (73,), 11: (64,), 13: (74,)}
 
 
 def kernel(n_ctx, qp_ref, kvp_ref, qr_ref, kvr_ref, doc_ref, span_ref, op_ref, or_ref, *scratch):
@@ -181,7 +180,7 @@
             qa[g * TOK:(g + 1) * TOK, HD:] = abias[b]
         s = lax.dot_general(qa[...], kaug[b], (((1,), (1,)), ((), ())), preferred_element_type=F32)
         causal = lax.broadcasted_iota(jnp.int32, (TOK, TOK), 1) <= lax.broadcasted_iota(jnp.int32, (TOK, TOK), 0)
-        keep = i % 3
+        keep = b
         for g in range(GROUP):
             sg = s[g * TOK:(g + 1) * TOK]
             diag = jnp.where(causal, sg[:, KEYS - TOK:], -BIG)
@@ -209,7 +208,7 @@
                     at = inv[jnp.maximum(place - 16 + t, 0)]
                     vaug[t * TOK:(t + 1) * TOK, :HD] = kvb[sig][at]
 
-        o = lax.dot_general(pbuf[i % 3], vaug[...], (((1,), (0,)), ((), ())), preferred_element_type=F32)
+        o = lax.dot_general(pbuf[b], vaug[...], (((1,), (0,)), ((), ())), preferred_element_type=F32)
         o = (o[:, :HD] / o[:, HD:]).astype(BF)
         for g in range(GROUP):
             obuf[i, :, g * HD:(g + 1) * HD] = o[g * TOK:(g + 1) * TOK]
@@ -229,29 +228,23 @@
                 def _(o_ref=o_ref):
                     pltpu.make_async_copy(obuf.at[i], o_ref.at[:, cols], olocal.at[j]).start()
 
-    @pl.loop(0, 10)
-    def _(i):
-        for k, items in BEFORE_S.items():
-            if items:
-                @pl.when(i == k)
-                def _(items=items):
-                    for item in items:
-                        tick(item // 10, item % 10)
-
-        @pl.when(i < 8)
+    @pl.loop(0, 4 * HK)
+    def _(step):
+        for k, items in BEFORE.items():
+            @pl.when(step == k)
+            def _(items=items):
+                for item in items:
+                    tick(item // 10, item % 10)
+
+        i = step // 4 * 2 + step % 2
+
+        @pl.when(step % 4 < 2)
         def _():
             scores(i)
 
-        for k, items in BEFORE_P.items():
-            if items:
-                @pl.when(i == k)
-                def _(items=items):
-                    for item in items:
-                        tick(item // 10, item % 10)
-
-        @pl.when(i >= 2)
+        @pl.when(step % 4 >= 2)
         def _():
-            values(i - 2)
+            values(i)
 
     for j in range(HK):
         part = obuf.at[j]
@@ -283,7 +276,7 @@
             pltpu.VMEM((2, TOK, HK * GROUP * HD), BF),
             pltpu.VMEM((2, KEYS, 2 * HD), BF),
             pltpu.VMEM((KEYS, 2 * HD), BF),
-            pltpu.VMEM((3, ROWS, KEYS), BF),
+            pltpu.VMEM((2, ROWS, KEYS), BF),
             pltpu.VMEM((ROWS, 2 * HD), BF),
             pltpu.VMEM((2, TOK, HD), BF),
             pltpu.VMEM((NBLK + 16, TOK, HD), BF),

time: 69.3 us -> 68.3 us (0.986)
  Pallas kernels: 65.7 us -> 64.7 us
    pallas_call x1, Pallas kernels: 65.7 us -> 64.7 us  [on_device(): pl.pallas_call(functools.partial(kernel, n_ctx), out_shape=[jax.ShapeDtyp...]
where the time goes in v3:
time: 68.3 us; the launch traced here: 68.2 us
  Pallas kernels  64.7 us (95%)
  local copies, waits for them, and re-layouts  2.87 us (4%)
    pallas_call x1, Pallas kernels, on_device(): pl.pallas_call(functools.partial(kernel, n_ctx), out_shape=[jax.ShapeDtyp...  64.7 us
    unnamed x4, local copies, waits for them, and re-layouts  2.87 us

profile of v3, /device:TPU:1, one launch (start us, length us, event | category | flops | bytes accessed | tf_op | source)
XLA Modules:
  0.0 68.2 jit_solution(6196662525770937464)
XLA Ops:
  0.6 64.7 %shard_map.77 = (bf16[128,2560]{1,0:T(8,128)(2,1)}, bf16[128,2560]{1,0:T(8,128)(2,1)}) custom-call(bf16[128,2560]{1,0:T(8,128)(2,1)} %qp_ref.1, bf16[128,1024]{1,0:T(8,128)(2,1)} %kvp_ref.1, bf16[128,2560]{1,0:T(8,128)(2,1)} %qr_ref.1, bf16[128,1024]{1,0:T(8,128)(2,1)} %kvr_ref.1, s32[8]{0:T(128)} %doc_ref.1, s32[32]{0:T(128)} %span_ref.1), custom_call_target="tpu_custom_call" | custom-call | flops 6000000000 | bytes 4000000 | tf_op jit(solution)/shard_map/pallas_call | solution.py:269
  65.3 0.0 copy-start
  65.3 2.0 %copy.10 = bf16[128,2560]{1,0:T(8,128)(2,1)} copy(bf16[128,2560]{1,0:T(8,128)(2,1)} %get-tuple-element.4) | data formatting | bytes 1310720
  67.4 0.0 copy-done
  67.4 0.8 %copy.11 = bf16[128,2560]{1,0:T(8,128)(2,1)} copy(bf16[128,2560]{1,0:T(8,128)(2,1)S(1)} %copy-done) | data formatting | bytes 1310720
Async XLA Ops:
  65.3 2.0 %copy-start = (bf16[128,2560]{1,0:T(8,128)(2,1)S(1)}, bf16[128,2560]{1,0:T(8,128)(2,1)}, u32[]{:S(2)}) copy-start(bf16[128,2560]{1,0:T(8,128)(2,1)} %get-tuple-element.5) | copy-start | bytes 1966084

commit v4 on v3

--- a/solution.py
+++ b/solution.py
@@ -16,8 +16,10 @@
 BIG = 131072.0
 NSIG = 2 * HK
 BF, F32 = jnp.bfloat16, jnp.float32
+AHEAD, QUERIES_AT = 4, (4, 6, 9, 12)
 PROLOGUE = (0, 10, 20, 30, 1, 11, 21, 40, 2, 31, 12, 22, 3, 50, 13, 41, 23, 4, 60, 32)
 BEFORE = {1: (51, 42, 14), 2: (70,), 3: (33, 24, 61), 4: (52,), 5: (43, 71, 34), 6: (62,), 7: (44, 53), 8: (72,), 9: (63, 54), 10: (73,), 11: (64,), 13: (74,)}
+OWN_ORDER = tuple(k // 10 for k in PROLOGUE + sum(BEFORE.values(), ()) if k % 10 == 0)
 
 
 def kernel(n_ctx, qp_ref, kvp_ref, qr_ref, kvr_ref, doc_ref, span_ref, op_ref, or_ref, *scratch):
@@ -53,12 +55,18 @@
             pltpu.make_async_copy(kv_ref.at[:, kv_cols(sig)], kvb[sig].at[slot(z) + y], lk.at[sig]).start()
         pltpu.make_async_copy(q_ref, qbuf.at[1], lq).start()
 
-    def peer_copies(kv_ref, q_ref):
-        for sig in range(NSIG):
-            remote(kv_ref.at[:, kv_cols(sig)], kvb[sig].at[slot(z) + y], ys, yr.at[sig], peer_y).start()
-        for j in range(HK):
-            cols = pl.ds(j * GROUP * HD, GROUP * HD)
-            remote(q_ref.at[:, cols], qbuf.at[0, :, cols], yqs, yqr.at[j], peer_y).start()
+    def kv_send(sig):
+        for m, kv_ref in enumerate((kvr_ref, kvp_ref)):
+            @pl.when(y == m)
+            def _(kv_ref=kv_ref):
+                remote(kv_ref.at[:, kv_cols(sig)], kvb[sig].at[slot(z) + y], ys, yr.at[sig], peer_y).start()
+
+    def q_send(j):
+        cols = pl.ds(j * GROUP * HD, GROUP * HD)
+        for m, q_ref in enumerate((qr_ref, qp_ref)):
+            @pl.when(y == m)
+            def _(q_ref=q_ref):
+                remote(q_ref.at[:, cols], qbuf.at[0, :, cols], yqs, yqr.at[j], peer_y).start()
 
     @pl.when(y == 0)
     def _():
@@ -70,13 +78,8 @@
 
     pl.semaphore_wait(barrier, 4)
 
-    @pl.when(y == 0)
-    def _():
-        peer_copies(kvr_ref, qr_ref)
-
-    @pl.when(y == 1)
-    def _():
-        peer_copies(kvp_ref, qp_ref)
+    for sig in OWN_ORDER[:AHEAD]:
+        kv_send(sig)
 
     def tick(sig, d):
         buf = kvb[sig]
@@ -149,9 +152,13 @@
         return span_ref[source]
 
     for count, item in enumerate(PROLOGUE):
-        if count == 3:
+        if count == 4:
             tables()
         tick(item // 10, item % 10)
+        if AHEAD + count < NSIG:
+            kv_send(OWN_ORDER[AHEAD + count])
+        if count in QUERIES_AT:
+            q_send(QUERIES_AT.index(count))
     pltpu.make_async_copy(qbuf.at[1], qbuf.at[1], lq).wait()
 
     def scores(i):

time: 68.3 us -> 68.4 us (level)
  no operation moved by 1% of the time
where the time goes in v4:
time: 68.4 us; the launch traced here: 68.3 us
  Pallas kernels  64.8 us (95%)
  local copies, waits for them, and re-layouts  2.87 us (4%)
    pallas_call x1, Pallas kernels, on_device(): pl.pallas_call(functools.partial(kernel, n_ctx), out_shape=[jax.ShapeDtyp...  64.8 us
    unnamed x4, local copies, waits for them, and re-layouts  2.87 us

profile of v4, /device:TPU:1, one launch (start us, length us, event | category | flops | bytes accessed | tf_op | source)
XLA Modules:
  0.0 68.3 jit_solution(16846506101392004711)
XLA Ops:
  0.6 64.8 %shard_map.77 = (bf16[128,2560]{1,0:T(8,128)(2,1)}, bf16[128,2560]{1,0:T(8,128)(2,1)}) custom-call(bf16[128,2560]{1,0:T(8,128)(2,1)} %qp_ref.1, bf16[128,1024]{1,0:T(8,128)(2,1)} %kvp_ref.1, bf16[128,2560]{1,0:T(8,128)(2,1)} %qr_ref.1, bf16[128,1024]{1,0:T(8,128)(2,1)} %kvr_ref.1, s32[8]{0:T(128)} %doc_ref.1, s32[32]{0:T(128)} %span_ref.1), custom_call_target="tpu_custom_call" | custom-call | flops 6000000000 | bytes 4000000 | tf_op jit(solution)/shard_map/pallas_call | solution.py:276
  65.4 0.0 copy-start
  65.4 2.0 %copy.10 = bf16[128,2560]{1,0:T(8,128)(2,1)} copy(bf16[128,2560]{1,0:T(8,128)(2,1)} %get-tuple-element.4) | data formatting | bytes 1310720
  67.5 0.0 copy-done
  67.5 0.8 %copy.11 = bf16[128,2560]{1,0:T(8,128)(2,1)} copy(bf16[128,2560]{1,0:T(8,128)(2,1)S(1)} %copy-done) | data formatting | bytes 1310720
Async XLA Ops:
  65.4 2.0 %copy-start = (bf16[128,2560]{1,0:T(8,128)(2,1)S(1)}, bf16[128,2560]{1,0:T(8,128)(2,1)}, u32[]{:S(2)}) copy-start(bf16[128,2560]{1,0:T(8,128)(2,1)} %get-tuple-element.5) | copy-start | bytes 1966084
